TPU v7x, 256 devices: a whole 4x4x8 slice. The times are simulated.
256 devices in a mesh: pair: 2 (over core), rep: 32 (over z, x), slab: 4 (over y).
Axes of the slice: x: 4, y: 4, z: 8, core: 2. Of those that a mesh axis runs over, the one named last changes fastest.
Arguments:
- amplitudes: bfloat16 [16384, 4096], P(('pair', 'slab'), 'rep'), may hold values from -6 to 6
- tile_pairs: int32 [16384], P(('pair', 'slab')), may hold values from 0 to 15, as said below
- row_pairs: int32 [16384], P(('pair', 'slab')), may hold values from 0 to 255
- owner: int32 [16], replicated, may hold values from 0 to 15, as said below
- integrals: bfloat16 [2, 16, 4096, 4096], P(None, 'pair', 'rep', 'slab'), may hold values from -0.0625 to 0.0625
Outputs:
- ladder: bfloat16 [2048, 2, 4096], P(('pair', 'slab'), None, 'rep')
Inputs may be any that keep to these rules, and one draw needn't show every extreme that they name: Each occupied pair of a device is named by exactly 8 of its rows, with distinct tile pairs. Call slots p * 8 to (p + 1) * 8 - 1 owner block p. At most 6 tiles of one occupied pair have slots owner[tile_pairs] in one owner block; in the rows of one device at most 1536 do, and every device reaches 1536 for some block. `owner`: each value once.
All inputs are finite; a program needn't handle non-finite values.
Results may differ from a plain program's by a relative error of at most 0.001.
Values may be sent and summed in bfloat16 or wider, within the bound.
No kernel may reach another device: no remote copies, remote signals or barrier semaphores. Data moves between devices by JAX's collectives and lax.ppermute only.
A program may use at most 128 MiB of HBM per device.

v0:
```python
import jax
import jax.numpy as jnp
from jax import lax
from jax.sharding import PartitionSpec as P

PAIRS_DEV = 256


def body(amplitudes, tile_pairs, row_pairs, owner, integrals):
    groups = lax.axis_size("pair")
    tile_count = owner.shape[0]
    slot_width = tile_count // groups
    part_width = amplitudes.shape[1]
    lookup = tile_pairs[:, None] == jnp.arange(tile_count, dtype=jnp.int32)[None, :]
    slots = jnp.sum(jnp.where(lookup, owner[None, :], 0), axis=1)
    target = slots // slot_width
    local_slot = slots % slot_width
    place = (target * PAIRS_DEV + row_pairs) * slot_width + local_slot
    sendbuf = (
        jnp.zeros((groups * PAIRS_DEV * slot_width, part_width), jnp.bfloat16)
        .at[place]
        .set(amplitudes)
    )
    received = lax.all_to_all(
        sendbuf.reshape(groups, PAIRS_DEV * slot_width, part_width),
        "pair",
        split_axis=0,
        concat_axis=0,
        tiled=True,
    )
    operand = received.reshape(groups * PAIRS_DEV, slot_width * part_width)
    piece = lax.all_gather(integrals, "slab", axis=3, tiled=True)
    flat_piece = piece.reshape(piece.shape[0], -1, piece.shape[3])
    products = jnp.einsum("rk,ckn->rcn", operand, flat_piece, preferred_element_type=jnp.float32)
    partial_sum = lax.psum_scatter(products, "rep", scatter_dimension=2, tiled=True)
    result = lax.psum_scatter(partial_sum, "pair", scatter_dimension=0, tiled=True)
    return result.astype(jnp.bfloat16)


def solution(mesh):
    return jax.shard_map(
        body,
        mesh=mesh,
        in_specs=(
            P(("pair", "slab"), "rep"),
            P(("pair", "slab")),
            P(("pair", "slab")),
            P(),
            P(None, "pair", "rep", "slab"),
        ),
        out_specs=P(("pair", "slab"), None, "rep"),
        check_vma=False,
    )
```

profile of v0, /device:TPU:40, one launch (start us, length us, event | category | flops | bytes accessed | tf_op | source)
XLA Modules:
  0.0 452.6 jit_solution(795973035956883995)
XLA Ops:
  6.5 0.0 all-gather.2.cloned.1.call-start
  6.5 0.7 all-gather.2.cloned.1.call-update
  7.3 0.0 reduce-scatter.3.cloned.1.call-start
  7.3 0.8 select_reduce_fusion
  8.1 0.7 compare_select_fusion
  8.8 6.4 %scatter_custom_fusion = bf16[4096,128]{1,0:T(8,128)(2,1)S(1)} fusion(s32[2048]{0:T(1024)S(1)} %compare_select_fusion, bf16[2048,128]{1,0:T(8,128)(2,1)} %param.5, bf16[]{:T(256)} %constant.28.clone.1), kind=kCustom, calls=%fused_computation.1 | custom fusion | bytes 1049088 | tf_op jit(solution)/shard_map/scatter | solution.py:22
  15.2 4.6 %all_to_all.5 = bf16[2,2048,128]{2,1,0:T(8,128)(2,1)S(1)} all-to-all(bf16[2,2048,128]{2,1,0:T(8,128)(2,1)S(1)} %bitcast.5), channel_id=1, replica_groups=mesh['pair'=2,'rep'=32,'slab'=4] {'pair'}, dimensions={0} | all-to-all | bytes 2097152 | tf_op jit(solution)/shard_map/all_to_all | solution.py:24
  19.8 0.5 reshape.23
  20.3 148.0 %all-gather.2.cloned.1.call-done = bf16[2,8,128,4096]{3,2,1,0:T(8,128)(2,1)} async-done(((bf16[2,8,128,1024]{3,2,1,0:T(8,128)(2,1)}), bf16[2,8,128,4096]{3,2,1,0:T(8,128)(2,1)}) %all-gather.2.cloned.1.call-update) | async-done | bytes 16777232 | tf_op jit(solution)/shard_map/all_gather | solution.py:32
  168.3 15.6 %fusion.10 = f32[512,2,4096]{2,0,1:T(8,128)} fusion(bf16[512,1024,1]{1,0,2:T(8,128)(2,1)S(1)} %reshape.23, bf16[2,1024,4096]{2,1,0:T(8,128)(2,1)} %bitcast.6), kind=kOutput, calls=%fused_computation.20 | convolution fusion | flops 8589934592 | bytes 34603008 | tf_op jit(solution)/shard_map/rk,ckn->rcn/dot_general | solution.py:34
  183.9 0.0 reduce-scatter.3.cloned.1.call-update
  184.0 0.0 reduce-scatter.5.cloned.1.call-start
  184.0 245.1 %reduce-scatter.3.cloned.1.call-done = f32[512,2,128]{2,0,1:T(8,128)} async-done(((f32[512,2,4096]{2,0,1:T(8,128)}), f32[512,2,128]{2,0,1:T(8,128)}) %reduce-scatter.3.cloned.1.call-update) | async-done | bytes 524304 | tf_op jit(solution)/shard_map/reduce_scatter | solution.py:35
  429.1 0.0 reduce-scatter.5.cloned.1.call-update
  429.1 15.1 %reduce-scatter.5.cloned.1.call-done = f32[256,2,128]{2,0,1:T(8,128)} async-done(((f32[512,2,128]{2,0,1:T(8,128)}), f32[256,2,128]{2,0,1:T(8,128)}) %reduce-scatter.5.cloned.1.call-update) | async-done | bytes 262160 | tf_op jit(solution)/shard_map/reduce_scatter | solution.py:36
  444.3 1.0 convert_element_type.3
  445.2 0.8 copy.8
Async XLA Ops:
  6.5 161.8 %all-gather.2.cloned.1.call-start = ((), (), s32[]{:S(2)}) async-start(), calls=%async_computation.3 | async-start | bytes 20971520 | tf_op jit(solution)/shard_map/all_gather | solution.py:32
  7.3 421.8 %reduce-scatter.3.cloned.1.call-start = ((), (), s32[]{:S(2)}) async-start(), calls=%async_computation.4 | async-start | bytes 17301504 | tf_op jit(solution)/shard_map/reduce_scatter | solution.py:35
  184.0 260.3 %reduce-scatter.5.cloned.1.call-start = ((), (), s32[]{:S(2)}) async-start(), calls=%async_computation.5 | async-start | bytes 786432 | tf_op jit(solution)/shard_map/reduce_scatter | solution.py:36
Sparse Core Ops, SparseCore 0:
  9.2 159.1 all-gather.1
  184.1 244.9 reduce-scatter.2
  431.6 12.6 reduce-scatter.4
where the time goes:
time: 455 us; the launch traced here: 453 us
  waiting for transfers between devices  409 us (90%)
  matrix products  15.6 us (3%)
  between operations  13.1 us (3%)
  local copies, waits for them, and re-layouts  7.67 us (2%)
  blocking collectives  4.58 us (1%)
    reduce_scatter x1, waiting for transfers between devices, body(): lax.psum_scatter(products, 'rep', scatter_dimension=2, tiled=True)  245 us
    all_gather x1, waiting for transfers between devices, body(): piece = lax.all_gather(integrals, 'slab', axis=3, tiled=True)  148 us
    dot_general x1, matrix products, body(): jnp.einsum('rk,ckn->rcn', operand, flat_piece, preferred_element_type=jnp...  15.6 us
    reduce_scatter x1, waiting for transfers between devices, body(): lax.psum_scatter(partial_sum, 'pair', scatter_dimension=0, tiled=True)  15.1 us
  transfers between devices with their start and end apart: 3, of which 3 were waited for; matrix products, arithmetic and copies ran while one was open for 2% of the time, Pallas kernels for 0%

commit v1 on v0

v1 whole, which is shorter than its diff:
```python
import functools

import jax
import jax.numpy as jnp
from jax import lax
from jax.experimental import pallas as pl
from jax.experimental.pallas import tpu as pltpu
from jax.sharding import Mesh, PartitionSpec as P

PAIRS_DEV = 256
HALF = PAIRS_DEV // 2
FIRST = (0, 1)
SECOND = (3, 2)


def shift(value, axis, step):
    size = lax.axis_size(axis)
    return lax.ppermute(value, axis, [(i, (i + step) % size) for i in range(size)])


def products_kernel(x_ref, a_ref, own_ref, other_ref, o_ref, acc_ref, *, relative_first):
    depth = own_ref.shape[1]
    acc_ref[...] = jnp.dot(
        a_ref[0, :, :depth], own_ref[0], preferred_element_type=jnp.float32
    ) + jnp.dot(a_ref[0, :, depth:], other_ref[0], preferred_element_type=jnp.float32)
    for rel in range(4):
        column = pl.multiple_of(lax.rem(x_ref[0] + rel, 4) * 128, 128)
        for half in range(2):
            tile = acc_ref[half * HALF : (half + 1) * HALF, pl.ds(column, 128)]
            if relative_first:
                o_ref[rel, half, 0, 0, 0] = tile
            else:
                o_ref[half, 0, 0, rel, 0] = tile


def products(operand, own, other, x_index, relative_first):
    if relative_first:
        out_shape = (4, 2, 2, 2, 2, HALF, 128)
        out_block = (4, 2, 1, 1, 1, HALF, 128)
        out_map = lambda c, zl, d, x: (0, 0, d, zl, c, 0, 0)
    else:
        out_shape = (2, 2, 2, 4, 2, HALF, 128)
        out_block = (2, 1, 1, 4, 1, HALF, 128)
        out_map = lambda c, zl, d, x: (0, d, zl, 0, c, 0, 0)
    rows, contracted = operand.shape[1:]
    return pl.pallas_call(
        functools.partial(products_kernel, relative_first=relative_first),
        grid_spec=pltpu.PrefetchScalarGridSpec(
            num_scalar_prefetch=1,
            grid=(2, 2, 2),
            in_specs=[
                pl.BlockSpec((1, rows, contracted), lambda c, zl, d, x: (d, 0, 0)),
                pl.BlockSpec((1, contracted // 2, 512), lambda c, zl, d, x: (c, 0, zl)),
                pl.BlockSpec((1, contracted // 2, 512), lambda c, zl, d, x: (c, 0, zl)),
            ],
            out_specs=pl.BlockSpec(out_block, out_map),
            scratch_shapes=[pltpu.VMEM((rows, 512), jnp.float32)],
        ),
        out_shape=jax.ShapeDtypeStruct(out_shape, jnp.float32),
        compiler_params=pltpu.CompilerParams(vmem_limit_bytes=32 * 1024 * 1024),
        cost_estimate=pl.CostEstimate(
            flops=2 * 2 * rows * contracted * 2048, bytes_accessed=16 * 1024 * 1024, transcendentals=0
        ),
    )(x_index, operand, own, other)


def sum_over_x(tiles):
    from_left = shift(tiles[2, 0], "x", 1)
    from_right = shift(tiles[2, 1], "x", -1)
    left_late = shift(tiles[1, 1], "x", 1)
    right_late = shift(tiles[3, 0], "x", -1)
    left_early = shift(tiles[1, 0] + from_left, "x", 1)
    right_early = shift(tiles[3, 1] + from_right, "x", -1)
    first = tiles[0, 0] + left_early + right_late
    second = tiles[0, 1] + left_late + right_early
    return jnp.stack([first, second])


def sum_over_z(tiles):
    up = shift(tiles[4, 0], "z", 1)
    down = shift(tiles[4, 1], "z", -1)
    up = shift(tiles[3] + jnp.stack([up, jnp.zeros_like(up)]), "z", 1)
    down = shift(tiles[5] + jnp.stack([jnp.zeros_like(down), down]), "z", -1)
    up = shift(tiles[2] + up, "z", 1)
    down = shift(tiles[6] + down, "z", -1)
    up = shift(tiles[1] + up, "z", 1)
    down = shift(tiles[7] + down, "z", -1)
    return tiles[0] + up + down


def placements():
    moves = ([], [])
    for y in range(4):
        for z in range(8):
            upper, d, zl = z // 4, (z % 4) // 2, z % 2
            first_target = ((2 * y + zl) * 4) + (y + FIRST[d]) % 4
            second_target = ((2 * y + zl) * 4) + (y + SECOND[d]) % 4
            moves[upper].append((z * 4 + y, first_target))
            moves[1 - upper].append((z * 4 + y, second_target))
    return moves


def body(amplitudes, tile_pairs, row_pairs, owner, integrals):
    pair, x, z = lax.axis_index("pair"), lax.axis_index("x"), lax.axis_index("z")
    tile_count = owner.shape[0]
    slot_width = integrals.shape[1]
    part_width = amplitudes.shape[1]
    own = integrals.reshape(integrals.shape[0], slot_width * part_width, -1)
    other = shift(own, "pair", 1)

    lookup = tile_pairs[:, None] == jnp.arange(tile_count, dtype=jnp.int32)[None, :]
    slots = jnp.sum(jnp.where(lookup, owner[None, :], 0), axis=1)
    place = row_pairs * tile_count + (slots - pair * slot_width) % tile_count
    local = (
        jnp.zeros((PAIRS_DEV * tile_count, part_width), jnp.bfloat16).at[place].set(amplitudes)
    ).reshape(PAIRS_DEV, tile_count * part_width)
    after = shift(local, "slab", -1)
    before = shift(local, "slab", 1)
    across = jnp.concatenate(
        [shift(after[:HALF], "slab", -1), shift(before[HALF:], "slab", 1)]
    )

    x_index = x.astype(jnp.int32).reshape(1)
    first = products(jnp.stack([local, after]), own, other, x_index, False)
    second = products(jnp.stack([before, across]), own, other, x_index, True)

    first = lax.psum_scatter(
        first.reshape(8, 4 * 2 * HALF, 128), "z", scatter_dimension=0, tiled=True
    ).reshape(4, 2, HALF, 128)
    first = sum_over_x(first)

    second = sum_over_x(second)
    second = second[::-1].reshape(8, 2, HALF, 128)
    second = lax.dynamic_slice_in_dim(jnp.concatenate([second, second]), z, 8, 0)
    second = sum_over_z(second)

    first = first.astype(jnp.bfloat16)
    second = second.astype(jnp.bfloat16)
    low = z < 4
    moves = placements()
    top = lax.ppermute(jnp.where(low, first, second), ("z", "slab"), moves[0])
    bottom = lax.ppermute(jnp.where(low, second, first), ("z", "slab"), moves[1])
    return jnp.concatenate([top, bottom], axis=1).transpose(1, 0, 2)


def solution(mesh):
    fine = Mesh(mesh.devices.reshape(2, 8, 4, 4), ("pair", "z", "x", "slab"))
    return jax.shard_map(
        body,
        mesh=fine,
        in_specs=(
            P(("pair", "slab"), ("z", "x")),
            P(("pair", "slab")),
            P(("pair", "slab")),
            P(),
            P(None, "pair", ("z", "x"), "slab"),
        ),
        out_specs=P(("pair", "slab"), None, ("z", "x")),
        check_vma=False,
    )
```

time: 455 us -> 213 us (0.47)
  waiting for transfers between devices: 409 us -> 110 us
  starting transfers between devices: 0.08 us -> 45.3 us
  Pallas kernels: 0 us -> 18.9 us
  matrix products: 15.6 us -> 0 us
  local copies, waits for them, and re-layouts: 7.67 us -> 16.2 us
  blocking collectives: 4.58 us -> 0 us
    reduce_scatter x2 -> x1, waiting for transfers between devices: 260 us -> 0.01 us  [body(): lax.psum_scatter(first.reshape(8, 4 * 2 * HALF, 128), 'z', scatter_dimens...]
    all_gather x1 -> x0, waiting for transfers between devices: 148 us -> none  [body(): piece = lax.all_gather(integrals, 'slab', axis=3, tiled=True)]
    ppermute x0 -> x27, waiting for transfers between devices: none -> 110 us  [the longest x25 105 us: shift(): lax.ppermute(value, axis, [(i, (i + step) % size) for i in range(size)])]
    ppermute x0 -> x27, starting transfers between devices: none -> 45.3 us  [the longest x25 32.5 us: shift(): lax.ppermute(value, axis, [(i, (i + step) % size) for i in range(size)])]
    pallas_call x0 -> x2, Pallas kernels: none -> 18.9 us  [products(): pl.pallas_call(functools.partial(products_kernel, relative_first=relative...]
    dot_general x1 -> x0, matrix products: 15.6 us -> none  [body(): jnp.einsum('rk,ckn->rcn', operand, flat_piece, preferred_element_type=jnp...]
    unnamed x0 -> x8, local copies, waits for them, and re-layouts: none -> 5.97 us
    all_to_all x1 -> x0, blocking collectives: 4.58 us -> none  [body(): lax.all_to_all(sendbuf.reshape(groups, PAIRS_DEV * slot_width, part_width...]
  transfers between devices with their start and end apart: 3 -> 28, of which waited for: 3 -> 16; matrix products, arithmetic and copies ran while one was open for 2% -> 8% of each run, Pallas kernels for 0% -> 5%
where the time goes in v1:
time: 213 us; the launch traced here: 210 us
  waiting for transfers between devices  110 us (52%)
  starting transfers between devices  45.3 us (21%)
  Pallas kernels  18.9 us (9%)
  local copies, waits for them, and re-layouts  16.2 us (8%)
  between operations  13.6 us (6%)
  other arithmetic  6.45 us (3%)
    ppermute x25, waiting for transfers between devices, shift(): lax.ppermute(value, axis, [(i, (i + step) % size) for i in range(size)])  105 us
    ppermute x25, starting transfers between devices, shift(): lax.ppermute(value, axis, [(i, (i + step) % size) for i in range(size)])  32.5 us
    pallas_call x2, Pallas kernels, products(): pl.pallas_call(functools.partial(products_kernel, relative_first=relative...  18.9 us
    ppermute x1, starting transfers between devices, body(): lax.ppermute(jnp.where(low, second, first), ('z', 'slab'), moves[1])  9.44 us
    scatter x1, local copies, waits for them, and re-layouts, body(): jnp.zeros((PAIRS_DEV * tile_count, part_width), jnp.bfloat16).at[place]  6.41 us
    unnamed x8, local copies, waits for them, and re-layouts  5.97 us
    ppermute x1, waiting for transfers between devices, body(): top = lax.ppermute(jnp.where(low, first, second), ('z', 'slab'), moves[0])  4.91 us
  transfers between devices with their start and end apart: 28, of which 16 were waited for; matrix products, arithmetic and copies ran while one was open for 8% of the time, Pallas kernels for 5%

profile of v1, /device:TPU:40, one launch (start us, length us, event | category | flops | bytes accessed | tf_op | source)
XLA Modules:
  0.0 210.2 jit_solution(13280045083275971195)
XLA Ops:
  6.5 0.8 select_reduce_fusion
  8.1 6.4 %scatter_custom_fusion = bf16[4096,128]{1,0:T(8,128)(2,1)S(1)} fusion(s32[2048]{0:T(1024)S(1)} %compare_select_fusion, bf16[2048,128]{1,0:T(8,128)(2,1)} %param.5, bf16[]{:T(256)} %constant.36.clone.1), kind=kCustom, calls=%fused_computation.24 | custom fusion | bytes 1049088 | tf_op jit(solution)/shard_map/scatter | solution.py:115
  14.5 1.3 reshape.21
  16.7 24.8 %collective-permute-done = bf16[256,2048]{1,0:T(8,128)(2,1)S(1)} collective-permute-done((bf16[256,2048]{1,0:T(8,128)(2,1)}, bf16[256,2048]{1,0:T(8,128)(2,1)S(1)}, u32[]{:S(2)}, u32[]{:S(2)}) %collective-permute-start) | collective-permute-done | bytes 1048608 | tf_op jit(solution)/shard_map/ppermute | solution.py:18
  41.8 2.0 copy-done.2
  43.7 9.4 %shard_map.55 = f32[2,2,2,4,2,128,128]{6,5,4,3,2,1,0:T(8,128)S(1)} custom-call(s32[1]{0:T(128)} %bitcast.x_ref, bf16[2,256,2048]{2,1,0:T(8,128)(2,1)S(1)} %pad_maximum_fusion.a_ref, bf16[2,1024,1024]{2,1,0:T(8,128)(2,1)S(1)} %bitcast.128, bf16[2,1024,1024]{2,1,0:T(8,128)(2,1)} %collective-permute-done.1.other_ref), custom_call_target="tpu_custom_call" | custom-call | flops 4294967296 | bytes 16777216 | tf_op jit(solution)/shard_map/pallas_call | solution.py:46
  53.2 1.9 copy-done.1
  55.2 1.7 collective-permute-start.8
  56.8 23.4 %collective-permute-done.8 = bf16[256,2048]{1,0:T(8,128)(2,1)S(1)} collective-permute-done((bf16[256,2048]{1,0:T(8,128)(2,1)}, bf16[256,2048]{1,0:T(8,128)(2,1)S(1)}, u32[]{:S(2)}, u32[]{:S(2)}) %collective-permute-start.8) | collective-permute-done | bytes 1048608 | tf_op jit(solution)/shard_map/ppermute | solution.py:18
  80.3 1.8 collective-permute-start.10
  82.1 1.3 collective-permute-start.9
  83.4 11.1 %collective-permute-done.10 = bf16[128,2048]{1,0:T(8,128)(2,1)S(1)} collective-permute-done((bf16[128,2048]{1,0:T(8,128)(2,1)S(1)}, bf16[128,2048]{1,0:T(8,128)(2,1)S(1)}, u32[]{:S(2)}, u32[]{:S(2)}) %collective-permute-start.10) | collective-permute-done | bytes 524320 | tf_op jit(solution)/shard_map/ppermute | solution.py:18
  94.5 0.8 collective-permute-done.9
  95.6 2.0 copy-done.3
  97.7 9.5 %shard_map.56 = f32[4,2,2,2,2,128,128]{6,5,4,3,2,1,0:T(8,128)S(1)} custom-call(s32[1]{0:T(128)} %bitcast.x_ref, bf16[2,256,2048]{2,1,0:T(8,128)(2,1)S(1)} %pad_maximum_fusion.1.a_ref, bf16[2,1024,1024]{2,1,0:T(8,128)(2,1)S(1)} %bitcast.129, bf16[2,1024,1024]{2,1,0:T(8,128)(2,1)} %collective-permute-done.1.other_ref), custom_call_target="tpu_custom_call" | custom-call | flops 4294967296 | bytes 16777216 | tf_op jit(solution)/shard_map/pallas_call | solution.py:46
  107.3 1.6 collective-permute-start.11
  108.9 1.7 collective-permute-start.13
  110.6 1.5 collective-permute-start.15
  112.1 8.4 %collective-permute-done.11 = f32[2,2,2,128,128]{4,3,2,1,0:T(8,128)S(1)} collective-permute-done((f32[2,2,2,128,128]{4,3,2,1,0:T(8,128)S(1)}, f32[2,2,2,128,128]{4,3,2,1,0:T(8,128)S(1)}, u32[]{:S(2)}, u32[]{:S(2)}) %collective-permute-start.11) | collective-permute-done | bytes 524320 | tf_op jit(solution)/shard_map/ppermute | solution.py:18
  121.0 1.5 collective-permute-start.14
  122.5 1.3 collective-permute-done.13
  123.8 8.1 %collective-permute-done.15 = f32[2,2,2,128,128]{4,3,2,1,0:T(8,128)S(1)} collective-permute-done((f32[2,2,2,128,128]{4,3,2,1,0:T(8,128)S(1)}, f32[2,2,2,128,128]{4,3,2,1,0:T(8,128)S(1)}, u32[]{:S(2)}, u32[]{:S(2)}) %collective-permute-start.15) | collective-permute-done | bytes 524320 | tf_op jit(solution)/shard_map/ppermute | solution.py:18
  131.8 5.0 %collective-permute-done.12 = f32[2,2,2,128,128]{4,3,2,1,0:T(8,128)S(1)} collective-permute-done((f32[2,2,2,128,128]{4,3,2,1,0:T(8,128)S(1)}, f32[2,2,2,128,128]{4,3,2,1,0:T(8,128)S(1)}, u32[]{:S(2)}, u32[]{:S(2)}) %collective-permute-start.12) | collective-permute-done | bytes 524320 | tf_op jit(solution)/shard_map/ppermute | solution.py:18
  137.4 6.8 %collective-permute-done.14 = f32[2,2,2,128,128]{4,3,2,1,0:T(8,128)S(1)} collective-permute-done((f32[2,2,2,128,128]{4,3,2,1,0:T(8,128)S(1)}, f32[2,2,2,128,128]{4,3,2,1,0:T(8,128)S(1)}, u32[]{:S(2)}, u32[]{:S(2)}) %collective-permute-start.14) | collective-permute-done | bytes 524320 | tf_op jit(solution)/shard_map/ppermute | solution.py:18
  144.2 2.0 collective-permute-done.16
  146.2 1.1 fusion.4
  147.8 2.0 collective-permute-start.17
  149.8 2.8 %collective-permute-done.17 = f32[128,128]{1,0:T(8,128)S(1)} collective-permute-done((f32[128,128]{1,0:T(8,128)S(1)}, f32[128,128]{1,0:T(8,128)S(1)}, u32[]{:S(2)}, u32[]{:S(2)}) %collective-permute-start.17) | collective-permute-done | bytes 65568 | tf_op jit(solution)/shard_map/ppermute | solution.py:18
  152.6 1.6 collective-permute-start.18
  154.1 2.1 %collective-permute-start.21 = (f32[128,128]{1,0:T(8,128)S(1)}, f32[128,128]{1,0:T(8,128)S(1)}, u32[]{:S(2)}, u32[]{:S(2)}) collective-permute-start(f32[128,128]{1,0:T(8,128)S(1)} %get-tuple-element.16), channel_id=1, source_target_pairs={{0,112},{16,0},{32,16},{48,32},{64,48},{80,64},{96,80},{112,96},{1... | collective-permute-start | bytes 196616 | tf_op jit(solution)/shard_map/ppermute | solution.py:18
  156.2 2.9 %collective-permute-done.18 = f32[2,128,128]{2,1,0:T(8,128)S(1)} collective-permute-done((f32[2,128,128]{2,1,0:T(8,128)S(1)}, f32[2,128,128]{2,1,0:T(8,128)S(1)}, u32[]{:S(2)}, u32[]{:S(2)}) %collective-permute-start.18) | collective-permute-done | bytes 131104 | tf_op jit(solution)/shard_map/ppermute | solution.py:18
  159.4 1.0 slice_bitcast_fusion.22
  160.5 4.9 %collective-permute-done.19 = f32[2,128,128]{2,1,0:T(8,128)S(1)} collective-permute-done((f32[2,128,128]{2,1,0:T(8,128)S(1)}, f32[2,128,128]{2,1,0:T(8,128)S(1)}, u32[]{:S(2)}, u32[]{:S(2)}) %collective-permute-start.19) | collective-permute-done | bytes 131104 | tf_op jit(solution)/shard_map/ppermute | solution.py:18
  165.4 3.3 %collective-permute-start.22 = (f32[2,128,128]{2,1,0:T(8,128)S(1)}, f32[2,128,128]{2,1,0:T(8,128)S(1)}, u32[]{:S(2)}, u32[]{:S(2)}) collective-permute-start(f32[2,128,128]{2,1,0:T(8,128)S(1)} %get-tuple-element.14), channel_id=1, source_target_pairs={{0,112},{16,0},{32,16},{48,32},{64,48},{80,64},{96,80},{112,96},{1... | collective-permute-start | bytes 393224 | tf_op jit(solution)/shard_map/ppermute | solution.py:18
  168.7 1.5 collective-permute-start.4
  170.3 0.9 fusion.24
  171.1 2.1 collective-permute-start.3
  173.2 2.1 collective-permute-start.23
  175.8 0.9 collective-permute-done.3
  176.7 0.9 fusion.28
  177.6 2.0 collective-permute-start.7
  179.6 2.6 %collective-permute-start.24 = (f32[2,128,128]{2,1,0:T(8,128)S(1)}, f32[2,128,128]{2,1,0:T(8,128)S(1)}, u32[]{:S(2)}, u32[]{:S(2)}) collective-permute-start(f32[2,128,128]{2,1,0:T(8,128)S(1)} %fusion.13), channel_id=1, source_target_pairs={{0,112},{16,0},{32,16},{48,32},{64,48},{80,64},{96,80},{112,96},{1... | collective-permute-start | bytes 393224 | tf_op jit(solution)/shard_map/ppermute | solution.py:18
  182.1 0.9 fusion.29
  183.0 1.6 collective-permute-done.24
  184.7 9.4 %collective-permute-start.26 = (bf16[2,128,128]{2,1,0:T(8,128)(2,1)S(1)}, bf16[2,128,128]{2,1,0:T(8,128)(2,1)S(1)}, u32[]{:S(2)}, u32[]{:S(2)}) collective-permute-start(bf16[2,128,128]{2,1,0:T(8,128)(2,1)S(1)} %broadcast_select_fusion), channel_id=1, source_target_pairs={{0,3},{16,19},{32,2},{48,18},{64,0},{80,16},{96,1},{112,17},{1,32}... | collective-permute-start | bytes 196616 | tf_op jit(solution)/shard_map/ppermute | solution.py:142
  194.2 3.4 %collective-permute-start.25 = (bf16[2,128,128]{2,1,0:T(8,128)(2,1)S(1)}, bf16[2,128,128]{2,1,0:T(8,128)(2,1)S(1)}, u32[]{:S(2)}, u32[]{:S(2)}) collective-permute-start(bf16[2,128,128]{2,1,0:T(8,128)(2,1)S(1)} %get-tuple-element.5), channel_id=1, source_target_pairs={{0,0},{16,16},{32,1},{48,17},{64,3},{80,19},{96,2},{112,18},{1,33}... | collective-permute-start | bytes 196616 | tf_op jit(solution)/shard_map/ppermute | solution.py:141
  197.6 4.9 %collective-permute-done.25 = bf16[2,128,128]{2,1,0:T(8,128)(2,1)S(1)} collective-permute-done((bf16[2,128,128]{2,1,0:T(8,128)(2,1)S(1)}, bf16[2,128,128]{2,1,0:T(8,128)(2,1)S(1)}, u32[]{:S(2)}, u32[]{:S(2)}) %collective-permute-start.25) | collective-permute-done | bytes 65568 | tf_op jit(solution)/shard_map/ppermute | solution.py:141
  202.6 0.8 copy.12
  (50 shorter events, 4.9 us)
Async XLA Ops:
  6.5 152.9 %reduce-scatter.2.cloned.1.call-start = ((), (), s32[]{:S(2)}) async-start(), calls=%async_computation.1 | async-start | bytes 4718592 | tf_op jit(solution)/shard_map/reduce_scatter | solution.py:127
  6.5 35.2 %collective-permute-start.1 = (bf16[2,1024,1024]{2,1,0:T(8,128)(2,1)}, bf16[2,1024,1024]{2,1,0:T(8,128)(2,1)}, u32[]{:S(2)}, u32[]{:S(2)}) collective-permute-start(bf16[2,1024,1024]{2,1,0:T(8,128)(2,1)} %bitcast.127), channel_id=1, source_target_pairs={{0,128},{128,0},{1,129},{129,1},{2,130},{130,2},{3,131},{131,3},{4... | collective-permute-start | bytes 12582920 | tf_op jit(solution)/shard_map/ppermute | solution.py:18
  15.8 25.8 %collective-permute-start = (bf16[256,2048]{1,0:T(8,128)(2,1)}, bf16[256,2048]{1,0:T(8,128)(2,1)S(1)}, u32[]{:S(2)}, u32[]{:S(2)}) collective-permute-start(bf16[256,2048]{1,0:T(8,128)(2,1)} %reshape.21), channel_id=1, source_target_pairs={{0,3},{1,0},{2,1},{3,2},{4,7},{5,4},{6,5},{7,6},{8,11},{9,8},{10,9... | collective-permute-start | bytes 3145736 | tf_op jit(solution)/shard_map/ppermute | solution.py:18
  41.5 2.2 %copy-start.2 = (bf16[2,8,128,1024]{3,2,1,0:T(8,128)(2,1)S(1)}, bf16[2,8,128,1024]{3,2,1,0:T(8,128)(2,1)}, u32[]{:S(2)}) copy-start(bf16[2,8,128,1024]{3,2,1,0:T(8,128)(2,1)} %param.9) | copy-start | bytes 12582916
  53.2 2.0 copy-start.1
  55.2 25.1 %collective-permute-start.8 = (bf16[256,2048]{1,0:T(8,128)(2,1)}, bf16[256,2048]{1,0:T(8,128)(2,1)S(1)}, u32[]{:S(2)}, u32[]{:S(2)}) collective-permute-start(bf16[256,2048]{1,0:T(8,128)(2,1)} %reshape.21), channel_id=1, source_target_pairs={{0,1},{1,2},{2,3},{3,0},{4,5},{5,6},{6,7},{7,4},{8,9},{9,10},{10,1... | collective-permute-start | bytes 3145736 | tf_op jit(solution)/shard_map/ppermute | solution.py:18
  80.3 14.3 %collective-permute-start.10 = (bf16[128,2048]{1,0:T(8,128)(2,1)S(1)}, bf16[128,2048]{1,0:T(8,128)(2,1)S(1)}, u32[]{:S(2)}, u32[]{:S(2)}) collective-permute-start(bf16[128,2048]{1,0:T(8,128)(2,1)S(1)} %slice.117), channel_id=1, source_target_pairs={{0,1},{1,2},{2,3},{3,0},{4,5},{5,6},{6,7},{7,4},{8,9},{9,10},{10,1... | collective-permute-start | bytes 1572872 | tf_op jit(solution)/shard_map/ppermute | solution.py:18
  82.1 13.2 %collective-permute-start.9 = (bf16[128,2048]{1,0:T(8,128)(2,1)S(1)}, bf16[128,2048]{1,0:T(8,128)(2,1)S(1)}, u32[]{:S(2)}, u32[]{:S(2)}) collective-permute-start(bf16[128,2048]{1,0:T(8,128)(2,1)S(1)} %slice.116), channel_id=1, source_target_pairs={{0,3},{1,0},{2,1},{3,2},{4,7},{5,4},{6,5},{7,6},{8,11},{9,8},{10,9... | collective-permute-start | bytes 1572872 | tf_op jit(solution)/shard_map/ppermute | solution.py:18
  95.4 2.2 %copy-start.3 = (bf16[2,8,128,1024]{3,2,1,0:T(8,128)(2,1)S(1)}, bf16[2,8,128,1024]{3,2,1,0:T(8,128)(2,1)}, u32[]{:S(2)}) copy-start(bf16[2,8,128,1024]{3,2,1,0:T(8,128)(2,1)} %param.9) | copy-start | bytes 12582916
  107.1 29.6 %copy-start = (f32[4,2,2,2,2,128,128]{6,5,4,3,2,1,0:T(8,128)}, f32[4,2,2,2,2,128,128]{6,5,4,3,2,1,0:T(8,128)S(1)}, u32[]{:S(2)}) copy-start(f32[4,2,2,2,2,128,128]{6,5,4,3,2,1,0:T(8,128)S(1)} %shard_map.56) | copy-start | bytes 12582916
  107.3 13.2 %collective-permute-start.11 = (f32[2,2,2,128,128]{4,3,2,1,0:T(8,128)S(1)}, f32[2,2,2,128,128]{4,3,2,1,0:T(8,128)S(1)}, u32[]{:S(2)}, u32[]{:S(2)}) collective-permute-start(f32[2,2,2,128,128]{4,3,2,1,0:T(8,128)S(1)} %get-tuple-element.9), channel_id=1, source_target_pairs={{0,4},{4,8},{8,12},{12,0},{1,5},{5,9},{9,13},{13,1},{2,6},{6,10},{... | collective-permute-start | bytes 1572872 | tf_op jit(solution)/shard_map/ppermute | solution.py:18
  108.9 14.9 %collective-permute-start.13 = (f32[2,2,2,128,128]{4,3,2,1,0:T(8,128)S(1)}, f32[2,2,2,128,128]{4,3,2,1,0:T(8,128)S(1)}, u32[]{:S(2)}, u32[]{:S(2)}) collective-permute-start(f32[2,2,2,128,128]{4,3,2,1,0:T(8,128)S(1)} %get-tuple-element.12), channel_id=1, source_target_pairs={{0,12},{4,0},{8,4},{12,8},{1,13},{5,1},{9,5},{13,9},{2,14},{6,2},{... | collective-permute-start | bytes 1572872 | tf_op jit(solution)/shard_map/ppermute | solution.py:18
  110.6 21.2 %collective-permute-start.15 = (f32[2,2,2,128,128]{4,3,2,1,0:T(8,128)S(1)}, f32[2,2,2,128,128]{4,3,2,1,0:T(8,128)S(1)}, u32[]{:S(2)}, u32[]{:S(2)}) collective-permute-start(f32[2,2,2,128,128]{4,3,2,1,0:T(8,128)S(1)} %get-tuple-element.10), channel_id=1, source_target_pairs={{0,12},{4,0},{8,4},{12,8},{1,13},{5,1},{9,5},{13,9},{2,14},{6,2},{... | collective-permute-start | bytes 1572872 | tf_op jit(solution)/shard_map/ppermute | solution.py:18
  120.6 16.1 %collective-permute-start.12 = (f32[2,2,2,128,128]{4,3,2,1,0:T(8,128)S(1)}, f32[2,2,2,128,128]{4,3,2,1,0:T(8,128)S(1)}, u32[]{:S(2)}, u32[]{:S(2)}) collective-permute-start(f32[2,2,2,128,128]{4,3,2,1,0:T(8,128)S(1)} %fusion.5), channel_id=1, source_target_pairs={{0,4},{4,8},{8,12},{12,0},{1,5},{5,9},{9,13},{13,1},{2,6},{6,10},{... | collective-permute-start | bytes 1572872 | tf_op jit(solution)/shard_map/ppermute | solution.py:18
  121.0 23.2 %collective-permute-start.14 = (f32[2,2,2,128,128]{4,3,2,1,0:T(8,128)S(1)}, f32[2,2,2,128,128]{4,3,2,1,0:T(8,128)S(1)}, u32[]{:S(2)}, u32[]{:S(2)}) collective-permute-start(f32[2,2,2,128,128]{4,3,2,1,0:T(8,128)S(1)} %get-tuple-element.11), channel_id=1, source_target_pairs={{0,4},{4,8},{8,12},{12,0},{1,5},{5,9},{9,13},{13,1},{2,6},{6,10},{... | collective-permute-start | bytes 1572872 | tf_op jit(solution)/shard_map/ppermute | solution.py:18
  137.0 9.3 %collective-permute-start.16 = (f32[2,2,2,128,128]{4,3,2,1,0:T(8,128)S(1)}, f32[2,2,2,128,128]{4,3,2,1,0:T(8,128)S(1)}, u32[]{:S(2)}, u32[]{:S(2)}) collective-permute-start(f32[2,2,2,128,128]{4,3,2,1,0:T(8,128)S(1)} %get-tuple-element.8), channel_id=1, source_target_pairs={{0,12},{4,0},{8,4},{12,8},{1,13},{5,1},{9,5},{13,9},{2,14},{6,2},{... | collective-permute-start | bytes 1572872 | tf_op jit(solution)/shard_map/ppermute | solution.py:18
  147.8 4.8 %collective-permute-start.17 = (f32[128,128]{1,0:T(8,128)S(1)}, f32[128,128]{1,0:T(8,128)S(1)}, u32[]{:S(2)}, u32[]{:S(2)}) collective-permute-start(f32[128,128]{1,0:T(8,128)S(1)} %get-tuple-element.15), channel_id=1, source_target_pairs={{0,16},{16,32},{32,48},{48,64},{64,80},{80,96},{96,112},{112,0},{1... | collective-permute-start | bytes 196616 | tf_op jit(solution)/shard_map/ppermute | solution.py:18
  152.6 6.5 %collective-permute-start.18 = (f32[2,128,128]{2,1,0:T(8,128)S(1)}, f32[2,128,128]{2,1,0:T(8,128)S(1)}, u32[]{:S(2)}, u32[]{:S(2)}) collective-permute-start(f32[2,128,128]{2,1,0:T(8,128)S(1)} %fusion.14), channel_id=1, source_target_pairs={{0,16},{16,32},{32,48},{48,64},{64,80},{80,96},{96,112},{112,0},{1... | collective-permute-start | bytes 393224 | tf_op jit(solution)/shard_map/ppermute | solution.py:18
  154.1 6.3 %collective-permute-start.21 = (f32[128,128]{1,0:T(8,128)S(1)}, f32[128,128]{1,0:T(8,128)S(1)}, u32[]{:S(2)}, u32[]{:S(2)}) collective-permute-start(f32[128,128]{1,0:T(8,128)S(1)} %get-tuple-element.16), channel_id=1, source_target_pairs={{0,112},{16,0},{32,16},{48,32},{64,48},{80,64},{96,80},{112,96},{1... | collective-permute-start | bytes 196616 | tf_op jit(solution)/shard_map/ppermute | solution.py:18
  159.1 6.3 %collective-permute-start.19 = (f32[2,128,128]{2,1,0:T(8,128)S(1)}, f32[2,128,128]{2,1,0:T(8,128)S(1)}, u32[]{:S(2)}, u32[]{:S(2)}) collective-permute-start(f32[2,128,128]{2,1,0:T(8,128)S(1)} %fusion.15), channel_id=1, source_target_pairs={{0,16},{16,32},{32,48},{48,64},{64,80},{80,96},{96,112},{112,0},{1... | collective-permute-start | bytes 393224 | tf_op jit(solution)/shard_map/ppermute | solution.py:18
  160.4 9.9 %collective-permute-start.2 = (f32[128,128]{1,0:T(8,128)S(1)}, f32[128,128]{1,0:T(8,128)S(1)}, u32[]{:S(2)}, u32[]{:S(2)}) collective-permute-start(f32[128,128]{1,0:T(8,128)S(1)} %get-tuple-element.19), channel_id=1, source_target_pairs={{0,4},{4,8},{8,12},{12,0},{1,5},{5,9},{9,13},{13,1},{2,6},{6,10},{... | collective-permute-start | bytes 196616 | tf_op jit(solution)/shard_map/ppermute | solution.py:18
  165.4 7.8 %collective-permute-start.22 = (f32[2,128,128]{2,1,0:T(8,128)S(1)}, f32[2,128,128]{2,1,0:T(8,128)S(1)}, u32[]{:S(2)}, u32[]{:S(2)}) collective-permute-start(f32[2,128,128]{2,1,0:T(8,128)S(1)} %get-tuple-element.14), channel_id=1, source_target_pairs={{0,112},{16,0},{32,16},{48,32},{64,48},{80,64},{96,80},{112,96},{1... | collective-permute-start | bytes 393224 | tf_op jit(solution)/shard_map/ppermute | solution.py:18
  168.7 14.3 %collective-permute-start.20 = (f32[2,128,128]{2,1,0:T(8,128)S(1)}, f32[2,128,128]{2,1,0:T(8,128)S(1)}, u32[]{:S(2)}, u32[]{:S(2)}) collective-permute-start(f32[2,128,128]{2,1,0:T(8,128)S(1)} %get-tuple-element.13), channel_id=1, source_target_pairs={{0,16},{16,32},{32,48},{48,64},{64,80},{80,96},{96,112},{112,0},{1... | collective-permute-start | bytes 393224 | tf_op jit(solution)/shard_map/ppermute | solution.py:18
  168.7 6.6 %collective-permute-start.4 = (f32[128,128]{1,0:T(8,128)S(1)}, f32[128,128]{1,0:T(8,128)S(1)}, u32[]{:S(2)}, u32[]{:S(2)}) collective-permute-start(f32[128,128]{1,0:T(8,128)S(1)} %get-tuple-element.22), channel_id=1, source_target_pairs={{0,12},{4,0},{8,4},{12,8},{1,13},{5,1},{9,5},{13,9},{2,14},{6,2},{... | collective-permute-start | bytes 196616 | tf_op jit(solution)/shard_map/ppermute | solution.py:18
  170.2 5.6 %collective-permute-start.6 = (f32[128,128]{1,0:T(8,128)S(1)}, f32[128,128]{1,0:T(8,128)S(1)}, u32[]{:S(2)}, u32[]{:S(2)}) collective-permute-start(f32[128,128]{1,0:T(8,128)S(1)} %get-tuple-element.20), channel_id=1, source_target_pairs={{0,12},{4,0},{8,4},{12,8},{1,13},{5,1},{9,5},{13,9},{2,14},{6,2},{... | collective-permute-start | bytes 196616 | tf_op jit(solution)/shard_map/ppermute | solution.py:18
  171.1 5.5 %collective-permute-start.3 = (f32[128,128]{1,0:T(8,128)S(1)}, f32[128,128]{1,0:T(8,128)S(1)}, u32[]{:S(2)}, u32[]{:S(2)}) collective-permute-start(f32[128,128]{1,0:T(8,128)S(1)} %fusion.24), channel_id=1, source_target_pairs={{0,4},{4,8},{8,12},{12,0},{1,5},{5,9},{9,13},{13,1},{2,6},{6,10},{... | collective-permute-start | bytes 196616 | tf_op jit(solution)/shard_map/ppermute | solution.py:18
  173.2 6.3 %collective-permute-start.23 = (f32[2,128,128]{2,1,0:T(8,128)S(1)}, f32[2,128,128]{2,1,0:T(8,128)S(1)}, u32[]{:S(2)}, u32[]{:S(2)}) collective-permute-start(f32[2,128,128]{2,1,0:T(8,128)S(1)} %fusion.12), channel_id=1, source_target_pairs={{0,112},{16,0},{32,16},{48,32},{64,48},{80,64},{96,80},{112,96},{1... | collective-permute-start | bytes 393224 | tf_op jit(solution)/shard_map/ppermute | solution.py:18
  175.3 6.8 %collective-permute-start.5 = (f32[128,128]{1,0:T(8,128)S(1)}, f32[128,128]{1,0:T(8,128)S(1)}, u32[]{:S(2)}, u32[]{:S(2)}) collective-permute-start(f32[128,128]{1,0:T(8,128)S(1)} %get-tuple-element.21), channel_id=1, source_target_pairs={{0,4},{4,8},{8,12},{12,0},{1,5},{5,9},{9,13},{13,1},{2,6},{6,10},{... | collective-permute-start | bytes 196616 | tf_op jit(solution)/shard_map/ppermute | solution.py:18
  177.6 4.6 %collective-permute-start.7 = (f32[128,128]{1,0:T(8,128)S(1)}, f32[128,128]{1,0:T(8,128)S(1)}, u32[]{:S(2)}, u32[]{:S(2)}) collective-permute-start(f32[128,128]{1,0:T(8,128)S(1)} %get-tuple-element.18), channel_id=1, source_target_pairs={{0,12},{4,0},{8,4},{12,8},{1,13},{5,1},{9,5},{13,9},{2,14},{6,2},{... | collective-permute-start | bytes 196616 | tf_op jit(solution)/shard_map/ppermute | solution.py:18
  179.6 5.1 %collective-permute-start.24 = (f32[2,128,128]{2,1,0:T(8,128)S(1)}, f32[2,128,128]{2,1,0:T(8,128)S(1)}, u32[]{:S(2)}, u32[]{:S(2)}) collective-permute-start(f32[2,128,128]{2,1,0:T(8,128)S(1)} %fusion.13), channel_id=1, source_target_pairs={{0,112},{16,0},{32,16},{48,32},{64,48},{80,64},{96,80},{112,96},{1... | collective-permute-start | bytes 393224 | tf_op jit(solution)/shard_map/ppermute | solution.py:18
  184.7 12.9 %collective-permute-start.26 = (bf16[2,128,128]{2,1,0:T(8,128)(2,1)S(1)}, bf16[2,128,128]{2,1,0:T(8,128)(2,1)S(1)}, u32[]{:S(2)}, u32[]{:S(2)}) collective-permute-start(bf16[2,128,128]{2,1,0:T(8,128)(2,1)S(1)} %broadcast_select_fusion), channel_id=1, source_target_pairs={{0,3},{16,19},{32,2},{48,18},{64,0},{80,16},{96,1},{112,17},{1,32}... | collective-permute-start | bytes 196616 | tf_op jit(solution)/shard_map/ppermute | solution.py:142
  194.2 8.4 %collective-permute-start.25 = (bf16[2,128,128]{2,1,0:T(8,128)(2,1)S(1)}, bf16[2,128,128]{2,1,0:T(8,128)(2,1)S(1)}, u32[]{:S(2)}, u32[]{:S(2)}) collective-permute-start(bf16[2,128,128]{2,1,0:T(8,128)(2,1)S(1)} %get-tuple-element.5), channel_id=1, source_target_pairs={{0,0},{16,16},{32,1},{48,17},{64,3},{80,19},{96,2},{112,18},{1,33}... | collective-permute-start | bytes 196616 | tf_op jit(solution)/shard_map/ppermute | solution.py:141
Sparse Core Ops, SparseCore 0:
  55.3 57.0 reduce-scatter.1

commit v2 on v1

v2 whole, which is shorter than its diff:
```python
import functools

import jax
import jax.numpy as jnp
from jax import lax
from jax.experimental import pallas as pl
from jax.experimental.pallas import tpu as pltpu
from jax.sharding import Mesh, PartitionSpec as P

PAIRS_DEV = 256
HALF = PAIRS_DEV // 2
DOMAIN = 8
LANES = 128
PACKED = (DOMAIN + 1) * LANES
FIRST = (0, 1)
SECOND = (3, 2)
MIB = 1024 * 1024


def shift(value, axis, step):
    size = lax.axis_size(axis)
    return lax.ppermute(value, axis, [(i, (i + step) % size) for i in range(size)])


def pack_kernel(owner_ref, base_ref, tile_ref, pair_ref, a_ref, o_ref):
    rows = a_ref.shape[0]
    count = owner_ref.shape[0]
    tiles = tile_ref[...]
    slots = jnp.zeros((1, rows), jnp.int32)
    for t in range(count):
        slots = jnp.where(tiles == t, owner_ref[t], slots)
    slots = lax.rem(slots - base_ref[0] + count, count)
    pairs = pair_ref[...]
    in_pair = lax.broadcasted_iota(jnp.int32, (PAIRS_DEV, rows), 0) == pairs
    in_slot = lax.broadcasted_iota(jnp.int32, (count, rows), 0) == slots
    pair_hot = in_pair.astype(jnp.float32).astype(jnp.bfloat16)
    slot_hot = in_slot.astype(jnp.float32)
    slot_hot_narrow = slot_hot.astype(jnp.bfloat16)
    contract_rows = (((1,), (1,)), ((), ()))
    present = lax.dot_general(
        pair_hot, slot_hot_narrow, contract_rows, preferred_element_type=jnp.float32
    )
    present_t = lax.dot_general(
        slot_hot_narrow, pair_hot, contract_rows, preferred_element_type=jnp.float32
    )
    row_id = lax.broadcasted_iota(jnp.int32, (count, count), 0)
    col_id = lax.broadcasted_iota(jnp.int32, (count, count), 1)
    upper = (row_id < col_id).astype(jnp.float32).astype(jnp.bfloat16)
    lower = (row_id > col_id).astype(jnp.float32).astype(jnp.bfloat16)
    before = jnp.dot(present.astype(jnp.bfloat16), upper, preferred_element_type=jnp.float32)
    before_t = jnp.dot(lower, present_t.astype(jnp.bfloat16), preferred_element_type=jnp.float32)
    by_row = jnp.dot(
        before_t.astype(jnp.bfloat16), pair_hot, preferred_element_type=jnp.float32
    )
    rank = jnp.sum(by_row * slot_hot, axis=0, keepdims=True).astype(jnp.int32)
    slot_id = lax.broadcasted_iota(jnp.int32, (PAIRS_DEV, count), 1).astype(jnp.float32)
    lane = lax.broadcasted_iota(jnp.int32, (PAIRS_DEV, LANES), 1)
    table = jnp.zeros((PAIRS_DEV, LANES), jnp.float32)
    pair_id = lax.broadcasted_iota(jnp.int32, (PAIRS_DEV, rows), 0)
    for i in range(DOMAIN):
        chosen = (pair_id == jnp.where(rank == i, pairs, -1)).astype(jnp.float32)
        o_ref[:, i * LANES : (i + 1) * LANES] = jnp.dot(
            chosen.astype(jnp.bfloat16), a_ref[...], preferred_element_type=jnp.float32
        ).astype(jnp.bfloat16)
        mine = jnp.where(before == i, present * slot_id, 0.0)
        table = jnp.where(lane == i, jnp.sum(mine, axis=1, keepdims=True), table)
    o_ref[:, DOMAIN * LANES :] = table.astype(jnp.bfloat16)


def pack(amplitudes, tile_pairs, row_pairs, owner, base):
    rows = amplitudes.shape[0]
    smem = pl.BlockSpec(memory_space=pltpu.SMEM)
    vmem = pl.BlockSpec(memory_space=pltpu.VMEM)
    return pl.pallas_call(
        pack_kernel,
        in_specs=[smem, smem, vmem, vmem, vmem],
        out_specs=vmem,
        out_shape=jax.ShapeDtypeStruct((PAIRS_DEV, PACKED), jnp.bfloat16),
        compiler_params=pltpu.CompilerParams(vmem_limit_bytes=32 * MIB),
        cost_estimate=pl.CostEstimate(flops=2 * rows * rows * LANES, bytes_accessed=2 * MIB, transcendentals=0),
    )(owner, base, tile_pairs.reshape(1, rows), row_pairs.reshape(1, rows), amplitudes)


def expand(piece, dense_ref, row):
    rows = piece.shape[0]
    count = dense_ref.shape[1] // LANES
    tiles = [piece[:, i * LANES : (i + 1) * LANES] for i in range(DOMAIN)]
    table = piece[:, DOMAIN * LANES :].astype(jnp.float32)
    slots = [jnp.broadcast_to(table[:, i : i + 1], (rows, LANES)) for i in range(DOMAIN)]
    for j in range(count):
        total = jnp.zeros((rows, LANES), jnp.bfloat16)
        for i in range(max(0, j - (count - DOMAIN)), min(DOMAIN - 1, j) + 1):
            mask = (slots[i] == j).astype(jnp.float32).astype(jnp.bfloat16)
            total = total + mask * tiles[i]
        dense_ref[row : row + rows, j * LANES : (j + 1) * LANES] = total


def products_kernel(at_ref, *refs, pieces, blocks, by_z):
    piece_refs, (own_ref, other_ref, o_ref, dense_ref, acc_ref) = refs[:pieces], refs[pieces:]
    step, zl = pl.program_id(0), pl.program_id(1)

    @pl.when((step == 0) & (zl == 0))
    def _():
        row = 0
        for ref in piece_refs:
            for start in range(0, ref.shape[0], HALF):
                expand(ref[start : start + HALF, :], dense_ref, row)
                row += HALF

    depth = own_ref.shape[1]
    acc_ref[...] = jnp.dot(
        dense_ref[:, :depth], own_ref[0], preferred_element_type=jnp.float32
    ) + jnp.dot(dense_ref[:, depth:], other_ref[0], preferred_element_type=jnp.float32)
    x, z = at_ref[0], at_ref[1]
    for d in range(blocks):
        for half in range(2):
            at = (2 * d + half) * HALF
            for rel in range(4):
                if by_z:
                    column = pl.multiple_of(lax.rem(x + rel, 4) * LANES, LANES)
                    tile = acc_ref[at : at + HALF, pl.ds(column, LANES)]
                    away = lax.rem(4 * d + 2 * (1 - half) + zl - z + 8, 8)
                    o_ref[away // 2, 0, 0, rel] = tile
                else:
                    o_ref[rel, d, half, 0, 0] = acc_ref[at : at + HALF, rel * LANES : (rel + 1) * LANES]


def products(packed, own, other, at, by_z):
    rows = sum(piece.shape[0] for piece in packed)
    blocks = rows // PAIRS_DEV
    contracted = 2 * own.shape[1]
    if by_z:
        out_shape = (4, 2, 2, 4, HALF, LANES)
        out_block = (4, 1, 1, 4, HALF, LANES)
        out_map = lambda c, zl, at: (0, lax.rem(zl + at[1], 2), c, 0, 0, 0)
    else:
        out_shape = (4, blocks, 2, 2, 2, HALF, LANES)
        out_block = (4, blocks, 2, 1, 1, HALF, LANES)
        out_map = lambda c, zl, at: (0, 0, 0, zl, c, 0, 0)
    return pl.pallas_call(
        functools.partial(products_kernel, pieces=len(packed), blocks=blocks, by_z=by_z),
        grid_spec=pltpu.PrefetchScalarGridSpec(
            num_scalar_prefetch=1,
            grid=(2, 2),
            in_specs=[pl.BlockSpec(piece.shape, lambda c, zl, at: (0, 0)) for piece in packed]
            + [pl.BlockSpec((1, contracted // 2, 512), lambda c, zl, at: (c, 0, zl))] * 2,
            out_specs=pl.BlockSpec(out_block, out_map),
            scratch_shapes=[
                pltpu.VMEM((rows, contracted), jnp.bfloat16),
                pltpu.VMEM((rows, 512), jnp.float32),
            ],
        ),
        out_shape=jax.ShapeDtypeStruct(out_shape, jnp.float32),
        compiler_params=pltpu.CompilerParams(vmem_limit_bytes=(24 if by_z else 56) * MIB),
        cost_estimate=pl.CostEstimate(
            flops=2 * rows * contracted * 2048,
            bytes_accessed=8 * MIB + rows * 8192,
            transcendentals=0,
        ),
    )(at, *packed, own, other)


def sum_over_x(tiles):
    from_left = shift(tiles[2, 0], "x", 1)
    from_right = shift(tiles[2, 1], "x", -1)
    left = shift(tiles[1] + jnp.stack([from_left, jnp.zeros_like(from_left)]), "x", 1)
    right = shift(tiles[3] + jnp.stack([jnp.zeros_like(from_right), from_right]), "x", -1)
    return tiles[0] + left + right


def sum_over_z(tiles):
    up = shift(tiles(4)[:2], "z", 1)
    down = shift(tiles(4)[2:], "z", -1)
    up = shift(tiles(3) + jnp.concatenate([up, jnp.zeros_like(up)]), "z", 1)
    down = shift(tiles(5) + jnp.concatenate([jnp.zeros_like(down), down]), "z", -1)
    up = shift(tiles(2) + up, "z", 1)
    down = shift(tiles(6) + down, "z", -1)
    up = shift(tiles(1) + up, "z", 1)
    down = shift(tiles(7) + down, "z", -1)
    return tiles(0) + up + down


def placements():
    moves = ([], [])
    for y in range(4):
        for z in range(8):
            d, bit, zl = z // 4, (z % 4) // 2, z % 2
            first_target = ((2 * y + zl) * 4) + (y + FIRST[d]) % 4
            second_target = ((2 * y + zl) * 4) + (y + SECOND[d]) % 4
            moves[bit].append((z * 4 + y, first_target))
            moves[1 - bit].append((z * 4 + y, second_target))
    return moves


def body(amplitudes, tile_pairs, row_pairs, owner, integrals):
    pair, x, z = lax.axis_index("pair"), lax.axis_index("x"), lax.axis_index("z")
    slot_width = integrals.shape[1]
    own = integrals.reshape(integrals.shape[0], slot_width * amplitudes.shape[1], -1)
    other = shift(own, "pair", 1)

    base = (pair * slot_width).astype(jnp.int32).reshape(1)
    local = pack(amplitudes, tile_pairs, row_pairs, owner, base)
    after = shift(local, "slab", -1)
    before = shift(local, "slab", 1)
    after, before = lax.optimization_barrier((after, before))
    across = [shift(after[:HALF], "slab", -1), shift(before[HALF:], "slab", 1)]

    at = jnp.stack([x, z]).astype(jnp.int32)
    firsts = [
        lax.psum_scatter(
            products([piece], own, other, at, False).reshape(4, -1, LANES),
            "x",
            scatter_dimension=0,
            tiled=True,
        ).reshape(4, 2 * HALF, LANES)
        for piece in (local, after)
    ]
    second = products([before, *across], own, other, at, True)

    chains = [
        sum_over_z(lambda away, c=c: second[away // 2, away % 2, c]) for c in range(2)
    ]
    second = sum_over_x(jnp.stack(chains, axis=1))
    first = lax.psum_scatter(
        jnp.concatenate(firsts), "z", scatter_dimension=0, tiled=True
    ).reshape(2, HALF, LANES)

    first = first.astype(jnp.bfloat16)
    second = second.astype(jnp.bfloat16)
    even = (z // 2) % 2 == 0
    moves = placements()
    top = lax.ppermute(jnp.where(even, first, second), ("z", "slab"), moves[0])
    bottom = lax.ppermute(jnp.where(even, second, first), ("z", "slab"), moves[1])
    return jnp.concatenate([top, bottom], axis=1).transpose(1, 0, 2)


def solution(mesh):
    fine = Mesh(mesh.devices.reshape(2, 8, 4, 4), ("pair", "z", "x", "slab"))
    return jax.shard_map(
        body,
        mesh=fine,
        in_specs=(
            P(("pair", "slab"), ("z", "x")),
            P(("pair", "slab")),
            P(("pair", "slab")),
            P(),
            P(None, "pair", ("z", "x"), "slab"),
        ),
        out_specs=P(("pair", "slab"), None, ("z", "x")),
        check_vma=False,
    )
```

time: 213 us -> 205 us (0.962); the launches traced: 210 us -> 205 us
  waiting for transfers between devices: 110 us -> 88.3 us
  Pallas kernels: 18.9 us -> 31.5 us
  starting transfers between devices: 45.3 us -> 57.3 us
  local copies, waits for them, and re-layouts: 16.2 us -> 6.23 us
    ppermute x25, waiting for transfers between devices: 105 us -> 77.5 us  [shift(): lax.ppermute(value, axis, [(i, (i + step) % size) for i in range(size)])]
    ppermute x25, starting transfers between devices: 32.5 us -> 46.4 us  [shift(): lax.ppermute(value, axis, [(i, (i + step) % size) for i in range(size)])]
    pallas_call x2 -> x4, Pallas kernels: 18.9 us -> 31.5 us  [the longest x3 27.7 us: products(): pl.pallas_call(functools.partial(products_kernel, pieces=len(packed), blo...]
    scatter x1 -> x0, local copies, waits for them, and re-layouts: 6.41 us -> none  [body(): jnp.zeros((PAIRS_DEV * tile_count, part_width), jnp.bfloat16).at[place]]
    ppermute x2, waiting for transfers between devices: 4.92 us -> 9.04 us  [the longest x1 7.77 us: body(): top = lax.ppermute(jnp.where(even, first, second), ('z', 'slab'), moves[0])]
    add x7 -> x11, other arithmetic: 1.03 us -> 4.42 us  [the longest x2 1.17 us: sum_over_z(): up = shift(tiles(1) + up, 'z', 1)]
    another operation x8 -> x1, other arithmetic: 3.61 us -> 0.58 us  [body(): at = jnp.stack([x, z]).astype(jnp.int32)]
    unnamed x8 -> x20, local copies, waits for them, and re-layouts: 5.97 us -> 5.34 us
  transfers between devices with their start and end apart: 28 -> 30, of which waited for: 16 -> 21; matrix products, arithmetic and copies ran while one was open for 8% -> 4% of each run, Pallas kernels for 5% -> 11%
where the time goes in v2:
time: 205 us
  waiting for transfers between devices  88.3 us (43%)
  starting transfers between devices  57.3 us (28%)
  Pallas kernels  31.5 us (15%)
  between operations  13.3 us (6%)
  other arithmetic  8.25 us (4%)
  local copies, waits for them, and re-layouts  6.23 us (3%)
    ppermute x25, waiting for transfers between devices, shift(): lax.ppermute(value, axis, [(i, (i + step) % size) for i in range(size)])  77.5 us
    ppermute x25, starting transfers between devices, shift(): lax.ppermute(value, axis, [(i, (i + step) % size) for i in range(size)])  46.4 us
    pallas_call x3, Pallas kernels, products(): pl.pallas_call(functools.partial(products_kernel, pieces=len(packed), blo...  27.7 us
    ppermute x1, starting transfers between devices, body(): lax.ppermute(jnp.where(even, second, first), ('z', 'slab'), moves[1])  8.88 us
    ppermute x1, waiting for transfers between devices, body(): top = lax.ppermute(jnp.where(even, first, second), ('z', 'slab'), moves[0])  7.77 us
    unnamed x20, local copies, waits for them, and re-layouts  5.34 us
  transfers between devices with their start and end apart: 30, of which 21 were waited for; matrix products, arithmetic and copies ran while one was open for 4% of the time, Pallas kernels for 11%

profile of v2, /device:TPU:40, one launch (start us, length us, event | category | flops | bytes accessed | tf_op | source)
XLA Modules:
  0.0 204.9 jit_solution(15621973454518634491)
XLA Ops:
  6.5 1.0 copy-done.4
  9.6 3.8 %shard_map.55.refs_0_ = bf16[256,1152]{1,0:T(8,128)(2,1)S(1)} custom-call(s32[16]{0:T(128)S(1)} %copy-done.7, s32[1]{0:T(128)} %bitcast.2.base_ref, s32[1,2048]{1,0:T(1,128)S(1)} %bitcast.110, s32[1,2048]{1,0:T(1,128)S(1)} %bitcast.111, bf16[2048,128]{1,0:T(8,128)(2,1)S(1)} %copy-done.4), custom_call_target="tpu_custom_call" | custom-call | flops 1073741824 | bytes 2097152 | tf_op jit(solution)/shard_map/pallas_call | solution.py:74
  14.0 1.6 collective-permute-start.2
  16.1 13.1 %collective-permute-done.1.refs_0_ = bf16[256,1152]{1,0:T(8,128)(2,1)S(1)} collective-permute-done((bf16[256,1152]{1,0:T(8,128)(2,1)S(1)}, bf16[256,1152]{1,0:T(8,128)(2,1)S(1)}, u32[]{:S(2)}, u32[]{:S(2)}) %collective-permute-start.1) | collective-permute-done | bytes 589856 | tf_op jit(solution)/shard_map/ppermute | solution.py:22
  29.3 1.4 collective-permute-done.2.refs_0_
  30.7 8.5 %shard_map.57 = f32[4,1,2,2,2,128,128]{6,5,4,3,2,1,0:T(8,128)} custom-call(s32[2]{0:T(128)} %pad_add_fusion.at_ref, bf16[256,1152]{1,0:T(8,128)(2,1)} %copy-done.8, bf16[2,1024,1024]{2,1,0:T(8,128)(2,1)} %bitcast.107, bf16[2,1024,1024]{2,1,0:T(8,128)(2,1)} %collective-permute-done.refs_2_.refs_4_), custom_call_target="tpu_custom_call" | custom-call | flops 2147483648 | bytes 10485760 | tf_op jit(solution)/shard_map/pallas_call | solution.py:140
  39.4 8.7 %shard_map.56 = f32[4,1,2,2,2,128,128]{6,5,4,3,2,1,0:T(8,128)} custom-call(s32[2]{0:T(128)} %pad_add_fusion.at_ref, bf16[256,1152]{1,0:T(8,128)(2,1)} %copy-done.2, bf16[2,1024,1024]{2,1,0:T(8,128)(2,1)} %bitcast.108, bf16[2,1024,1024]{2,1,0:T(8,128)(2,1)} %collective-permute-done.refs_2_.refs_4_), custom_call_target="tpu_custom_call" | custom-call | flops 2147483648 | bytes 10485760 | tf_op jit(solution)/shard_map/pallas_call | solution.py:140
  48.1 3.0 %collective-permute-start.3 = (bf16[128,1152]{1,0:T(8,128)(2,1)S(1)}, bf16[128,1152]{1,0:T(8,128)(2,1)S(1)}, u32[]{:S(2)}, u32[]{:S(2)}) collective-permute-start(bf16[128,1152]{1,0:T(8,128)(2,1)S(1)} %slice.97), channel_id=1, source_target_pairs={{0,3},{1,0},{2,1},{3,2},{4,7},{5,4},{6,5},{7,6},{8,11},{9,8},{10,9... | collective-permute-start | bytes 884744 | tf_op jit(solution)/shard_map/ppermute | solution.py:22
  51.5 5.5 %collective-permute-done.3.refs_1_ = bf16[128,1152]{1,0:T(8,128)(2,1)S(1)} collective-permute-done((bf16[128,1152]{1,0:T(8,128)(2,1)S(1)}, bf16[128,1152]{1,0:T(8,128)(2,1)S(1)}, u32[]{:S(2)}, u32[]{:S(2)}) %collective-permute-start.3) | collective-permute-done | bytes 294944 | tf_op jit(solution)/shard_map/ppermute | solution.py:22
  57.0 2.5 %collective-permute-done.4.refs_2_ = bf16[128,1152]{1,0:T(8,128)(2,1)S(1)} collective-permute-done((bf16[128,1152]{1,0:T(8,128)(2,1)S(1)}, bf16[128,1152]{1,0:T(8,128)(2,1)S(1)}, u32[]{:S(2)}, u32[]{:S(2)}) %collective-permute-start.4) | collective-permute-done | bytes 294944 | tf_op jit(solution)/shard_map/ppermute | solution.py:22
  59.5 2.2 %copy-done = bf16[2,8,128,1024]{3,2,1,0:T(8,128)(2,1)S(1)} copy-done((bf16[2,8,128,1024]{3,2,1,0:T(8,128)(2,1)S(1)}, bf16[2,8,128,1024]{3,2,1,0:T(8,128)(2,1)}, u32[]{:S(2)}) %copy-start) | copy-done | bytes 4194328
  61.7 10.5 %shard_map.58 = f32[4,2,2,4,128,128]{5,4,3,2,1,0:T(8,128)S(1)} custom-call(s32[2]{0:T(128)S(1)} %copy-done.3, bf16[256,1152]{1,0:T(8,128)(2,1)S(1)} %collective-permute-done.2.refs_0_, bf16[128,1152]{1,0:T(8,128)(2,1)S(1)} %collective-permute-done.3.refs_1_, bf16[128,1152]{1,0:T(8,128)(2,1)S(1)} %collective-permute-done.4.refs_2_, ...), custom_call_target="tpu_custom_call" | custom-call | flops 4294967296 | bytes 12582912 | tf_op jit(solution)/shard_map/pallas_call | solution.py:140
  72.3 2.0 collective-permute-start.5
  74.3 3.0 %collective-permute-done.5 = f32[2,128,128]{2,1,0:T(8,128)S(1)} collective-permute-done((f32[2,128,128]{2,1,0:T(8,128)S(1)}, f32[2,128,128]{2,1,0:T(8,128)S(1)}, u32[]{:S(2)}, u32[]{:S(2)}) %collective-permute-start.5) | collective-permute-done | bytes 131104 | tf_op jit(solution)/shard_map/ppermute | solution.py:22
  77.3 2.1 %collective-permute-start.6 = (f32[4,128,128]{2,1,0:T(8,128)S(1)}, f32[4,128,128]{2,1,0:T(8,128)S(1)}, u32[]{:S(2)}, u32[]{:S(2)}) collective-permute-start(f32[4,128,128]{2,1,0:T(8,128)S(1)} %fusion.11), channel_id=1, source_target_pairs={{0,16},{16,32},{32,48},{48,64},{64,80},{80,96},{96,112},{112,0},{1... | collective-permute-start | bytes 786440 | tf_op jit(solution)/shard_map/ppermute | solution.py:22
  79.4 6.3 %collective-permute-done.6 = f32[4,128,128]{2,1,0:T(8,128)S(1)} collective-permute-done((f32[4,128,128]{2,1,0:T(8,128)S(1)}, f32[4,128,128]{2,1,0:T(8,128)S(1)}, u32[]{:S(2)}, u32[]{:S(2)}) %collective-permute-start.6) | collective-permute-done | bytes 262176 | tf_op jit(solution)/shard_map/ppermute | solution.py:22
  86.4 2.8 %collective-permute-start.9 = (f32[2,128,128]{2,1,0:T(8,128)S(1)}, f32[2,128,128]{2,1,0:T(8,128)S(1)}, u32[]{:S(2)}, u32[]{:S(2)}) collective-permute-start(f32[2,128,128]{2,1,0:T(8,128)S(1)} %get-tuple-element.19), channel_id=1, source_target_pairs={{0,112},{16,0},{32,16},{48,32},{64,48},{80,64},{96,80},{112,96},{1... | collective-permute-start | bytes 393224 | tf_op jit(solution)/shard_map/ppermute | solution.py:22
  89.2 3.5 %collective-permute-done.9 = f32[2,128,128]{2,1,0:T(8,128)S(1)} collective-permute-done((f32[2,128,128]{2,1,0:T(8,128)S(1)}, f32[2,128,128]{2,1,0:T(8,128)S(1)}, u32[]{:S(2)}, u32[]{:S(2)}) %collective-permute-start.9) | collective-permute-done | bytes 131104 | tf_op jit(solution)/shard_map/ppermute | solution.py:22
  93.5 3.3 %collective-permute-start.10 = (f32[4,128,128]{2,1,0:T(8,128)S(1)}, f32[4,128,128]{2,1,0:T(8,128)S(1)}, u32[]{:S(2)}, u32[]{:S(2)}) collective-permute-start(f32[4,128,128]{2,1,0:T(8,128)S(1)} %get-tuple-element.15), channel_id=1, source_target_pairs={{0,112},{16,0},{32,16},{48,32},{64,48},{80,64},{96,80},{112,96},{1... | collective-permute-start | bytes 786440 | tf_op jit(solution)/shard_map/ppermute | solution.py:22
  96.8 6.8 %collective-permute-done.10 = f32[4,128,128]{2,1,0:T(8,128)S(1)} collective-permute-done((f32[4,128,128]{2,1,0:T(8,128)S(1)}, f32[4,128,128]{2,1,0:T(8,128)S(1)}, u32[]{:S(2)}, u32[]{:S(2)}) %collective-permute-start.10) | collective-permute-done | bytes 262176 | tf_op jit(solution)/shard_map/ppermute | solution.py:22
  103.7 2.4 %collective-permute-start.11 = (f32[4,128,128]{2,1,0:T(8,128)S(1)}, f32[4,128,128]{2,1,0:T(8,128)S(1)}, u32[]{:S(2)}, u32[]{:S(2)}) collective-permute-start(f32[4,128,128]{2,1,0:T(8,128)S(1)} %fusion.9), channel_id=1, source_target_pairs={{0,112},{16,0},{32,16},{48,32},{64,48},{80,64},{96,80},{112,96},{1... | collective-permute-start | bytes 786440 | tf_op jit(solution)/shard_map/ppermute | solution.py:22
  106.1 1.6 collective-permute-start.8
  107.6 6.8 %collective-permute-done.11 = f32[4,128,128]{2,1,0:T(8,128)S(1)} collective-permute-done((f32[4,128,128]{2,1,0:T(8,128)S(1)}, f32[4,128,128]{2,1,0:T(8,128)S(1)}, u32[]{:S(2)}, u32[]{:S(2)}) %collective-permute-start.11) | collective-permute-done | bytes 262176 | tf_op jit(solution)/shard_map/ppermute | solution.py:22
  114.5 1.8 collective-permute-start.12
  116.3 3.7 %collective-permute-start.17 = (f32[2,128,128]{2,1,0:T(8,128)S(1)}, f32[2,128,128]{2,1,0:T(8,128)S(1)}, u32[]{:S(2)}, u32[]{:S(2)}) collective-permute-start(f32[2,128,128]{2,1,0:T(8,128)S(1)} %get-tuple-element.17), channel_id=1, source_target_pairs={{0,112},{16,0},{32,16},{48,32},{64,48},{80,64},{96,80},{112,96},{1... | collective-permute-start | bytes 393224 | tf_op jit(solution)/shard_map/ppermute | solution.py:22
  119.9 4.9 %collective-permute-done.17 = f32[2,128,128]{2,1,0:T(8,128)S(1)} collective-permute-done((f32[2,128,128]{2,1,0:T(8,128)S(1)}, f32[2,128,128]{2,1,0:T(8,128)S(1)}, u32[]{:S(2)}, u32[]{:S(2)}) %collective-permute-start.17) | collective-permute-done | bytes 131104 | tf_op jit(solution)/shard_map/ppermute | solution.py:22
  125.0 4.8 %collective-permute-start.14 = (f32[4,128,128]{2,1,0:T(8,128)S(1)}, f32[4,128,128]{2,1,0:T(8,128)S(1)}, u32[]{:S(2)}, u32[]{:S(2)}) collective-permute-start(f32[4,128,128]{2,1,0:T(8,128)S(1)} %get-tuple-element.13), channel_id=1, source_target_pairs={{0,16},{16,32},{32,48},{48,64},{64,80},{80,96},{96,112},{112,0},{1... | collective-permute-start | bytes 786440 | tf_op jit(solution)/shard_map/ppermute | solution.py:22
  129.8 2.3 %pad_maximum_fusion = f32[8,256,128]{2,1,0:T(8,128)} fusion(f32[4,256,128]{2,1,0:T(8,128)} %bitcast.120, f32[4,256,128]{2,1,0:T(8,128)} %bitcast.121), kind=kLoop, calls=%fused_computation | loop fusion | flops 262144 | bytes 2097152 | tf_op jit(solution)/shard_map/concatenate | solution.py:225
  132.1 1.8 collective-permute-done.14
  134.9 4.1 %collective-permute-start.15 = (f32[4,128,128]{2,1,0:T(8,128)S(1)}, f32[4,128,128]{2,1,0:T(8,128)S(1)}, u32[]{:S(2)}, u32[]{:S(2)}) collective-permute-start(f32[4,128,128]{2,1,0:T(8,128)S(1)} %fusion.4), channel_id=1, source_target_pairs={{0,16},{16,32},{32,48},{48,64},{64,80},{80,96},{96,112},{112,0},{1... | collective-permute-start | bytes 786440 | tf_op jit(solution)/shard_map/ppermute | solution.py:22
  139.0 1.4 collective-permute-done.18
  140.4 2.5 %collective-permute-done.15 = f32[4,128,128]{2,1,0:T(8,128)S(1)} collective-permute-done((f32[4,128,128]{2,1,0:T(8,128)S(1)}, f32[4,128,128]{2,1,0:T(8,128)S(1)}, u32[]{:S(2)}, u32[]{:S(2)}) %collective-permute-start.15) | collective-permute-done | bytes 262176 | tf_op jit(solution)/shard_map/ppermute | solution.py:22
  142.9 1.1 fusion.5
  144.0 2.4 %collective-permute-start.19 = (f32[4,128,128]{2,1,0:T(8,128)S(1)}, f32[4,128,128]{2,1,0:T(8,128)S(1)}, u32[]{:S(2)}, u32[]{:S(2)}) collective-permute-start(f32[4,128,128]{2,1,0:T(8,128)S(1)} %get-tuple-element.21), channel_id=1, source_target_pairs={{0,112},{16,0},{32,16},{48,32},{64,48},{80,64},{96,80},{112,96},{1... | collective-permute-start | bytes 786440 | tf_op jit(solution)/shard_map/ppermute | solution.py:22
  146.6 6.7 %collective-permute-done.19 = f32[4,128,128]{2,1,0:T(8,128)S(1)} collective-permute-done((f32[4,128,128]{2,1,0:T(8,128)S(1)}, f32[4,128,128]{2,1,0:T(8,128)S(1)}, u32[]{:S(2)}, u32[]{:S(2)}) %collective-permute-start.19) | collective-permute-done | bytes 262176 | tf_op jit(solution)/shard_map/ppermute | solution.py:22
  153.3 1.0 fusion.2
  155.2 2.1 %collective-permute-start.21 = (f32[128,128]{1,0:T(8,128)S(1)}, f32[128,128]{1,0:T(8,128)S(1)}, u32[]{:S(2)}, u32[]{:S(2)}) collective-permute-start(f32[128,128]{1,0:T(8,128)S(1)} %slice_bitcast_fusion.19), channel_id=1, source_target_pairs={{0,4},{4,8},{8,12},{12,0},{1,5},{5,9},{9,13},{13,1},{2,6},{6,10},{... | collective-permute-start | bytes 196616 | tf_op jit(solution)/shard_map/ppermute | solution.py:22
  157.3 4.9 %collective-permute-done.20 = f32[4,128,128]{2,1,0:T(8,128)S(1)} collective-permute-done((f32[4,128,128]{2,1,0:T(8,128)S(1)}, f32[4,128,128]{2,1,0:T(8,128)S(1)}, u32[]{:S(2)}, u32[]{:S(2)}) %collective-permute-start.20) | collective-permute-done | bytes 262176 | tf_op jit(solution)/shard_map/ppermute | solution.py:22
  162.2 1.0 fusion.7
  163.3 2.6 %collective-permute-start.23 = (f32[128,128]{1,0:T(8,128)S(1)}, f32[128,128]{1,0:T(8,128)S(1)}, u32[]{:S(2)}, u32[]{:S(2)}) collective-permute-start(f32[128,128]{1,0:T(8,128)S(1)} %slice_bitcast_fusion.18), channel_id=1, source_target_pairs={{0,12},{4,0},{8,4},{12,8},{1,13},{5,1},{9,5},{13,9},{2,14},{6,2},{... | collective-permute-start | bytes 196616 | tf_op jit(solution)/shard_map/ppermute | solution.py:22
  165.9 1.9 collective-permute-done.23
  167.8 3.6 %collective-permute-start.24 = (f32[2,128,128]{2,1,0:T(8,128)S(1)}, f32[2,128,128]{2,1,0:T(8,128)S(1)}, u32[]{:S(2)}, u32[]{:S(2)}) collective-permute-start(f32[2,128,128]{2,1,0:T(8,128)S(1)} %get-tuple-element.23), channel_id=1, source_target_pairs={{0,12},{4,0},{8,4},{12,8},{1,13},{5,1},{9,5},{13,9},{2,14},{6,2},{... | collective-permute-start | bytes 393224 | tf_op jit(solution)/shard_map/ppermute | solution.py:22
  171.5 1.7 reduce-scatter.8.cloned.1.call-done
  174.1 3.5 %collective-permute-done.22 = f32[2,128,128]{2,1,0:T(8,128)S(1)} collective-permute-done((f32[2,128,128]{2,1,0:T(8,128)S(1)}, f32[2,128,128]{2,1,0:T(8,128)S(1)}, u32[]{:S(2)}, u32[]{:S(2)}) %collective-permute-start.22) | collective-permute-done | bytes 131104 | tf_op jit(solution)/shard_map/ppermute | solution.py:22
  177.7 8.9 %collective-permute-start.26 = (bf16[2,128,128]{2,1,0:T(8,128)(2,1)S(1)}, bf16[2,128,128]{2,1,0:T(8,128)(2,1)S(1)}, u32[]{:S(2)}, u32[]{:S(2)}) collective-permute-start(bf16[2,128,128]{2,1,0:T(8,128)(2,1)S(1)} %broadcast_select_fusion), channel_id=1, source_target_pairs={{0,3},{16,19},{32,0},{48,16},{64,2},{80,18},{96,1},{112,17},{1,32}... | collective-permute-start | bytes 196616 | tf_op jit(solution)/shard_map/ppermute | solution.py:233
  186.6 1.9 collective-permute-start.25
  188.5 1.3 collective-permute-done.26
  189.8 7.8 %collective-permute-done.25 = bf16[2,128,128]{2,1,0:T(8,128)(2,1)S(1)} collective-permute-done((bf16[2,128,128]{2,1,0:T(8,128)(2,1)S(1)}, bf16[2,128,128]{2,1,0:T(8,128)(2,1)S(1)}, u32[]{:S(2)}, u32[]{:S(2)}) %collective-permute-start.25) | collective-permute-done | bytes 65568 | tf_op jit(solution)/shard_map/ppermute | solution.py:232
  (62 shorter events, 9.3 us)
Async XLA Ops:
  6.5 123.3 %reduce-scatter.6.cloned.1.call-start = ((), (), s32[]{:S(2)}) async-start(), calls=%async_computation.4 | async-start | bytes 2621440 | tf_op jit(solution)/shard_map/reduce_scatter | solution.py:210
  6.5 24.2 %collective-permute-start = (bf16[2,1024,1024]{2,1,0:T(8,128)(2,1)}, bf16[2,1024,1024]{2,1,0:T(8,128)(2,1)}, u32[]{:S(2)}, u32[]{:S(2)}) collective-permute-start(bf16[2,1024,1024]{2,1,0:T(8,128)(2,1)} %bitcast.106), channel_id=1, source_target_pairs={{0,128},{128,0},{1,129},{129,1},{2,130},{130,2},{3,131},{131,3},{4... | collective-permute-start | bytes 12582920 | tf_op jit(solution)/shard_map/ppermute | solution.py:22
  6.5 1.0 copy-start.4
  7.6 0.7 copy-start.5
  8.3 0.7 copy-start.6
  9.0 0.7 copy-start.7
  13.4 25.8 %copy-start.2 = (bf16[256,1152]{1,0:T(8,128)(2,1)}, bf16[256,1152]{1,0:T(8,128)(2,1)S(1)}, u32[]{:S(2)}) copy-start(bf16[256,1152]{1,0:T(8,128)(2,1)S(1)} %shard_map.55.refs_0_) | copy-start | bytes 1769476
  13.5 15.8 %collective-permute-start.1 = (bf16[256,1152]{1,0:T(8,128)(2,1)S(1)}, bf16[256,1152]{1,0:T(8,128)(2,1)S(1)}, u32[]{:S(2)}, u32[]{:S(2)}) collective-permute-start(bf16[256,1152]{1,0:T(8,128)(2,1)S(1)} %shard_map.55.refs_0_), channel_id=1, source_target_pairs={{0,3},{1,0},{2,1},{3,2},{4,7},{5,4},{6,5},{7,6},{8,11},{9,8},{10,9... | collective-permute-start | bytes 1769480 | tf_op jit(solution)/shard_map/ppermute | solution.py:22
  14.0 16.7 %collective-permute-start.2 = (bf16[256,1152]{1,0:T(8,128)(2,1)S(1)}, bf16[256,1152]{1,0:T(8,128)(2,1)S(1)}, u32[]{:S(2)}, u32[]{:S(2)}) collective-permute-start(bf16[256,1152]{1,0:T(8,128)(2,1)S(1)} %shard_map.55.refs_0_), channel_id=1, source_target_pairs={{0,1},{1,2},{2,3},{3,0},{4,5},{5,6},{6,7},{7,4},{8,9},{9,10},{10,1... | collective-permute-start | bytes 1769480 | tf_op jit(solution)/shard_map/ppermute | solution.py:22
  29.3 1.4 copy-start.8
  39.3 8.8 %copy-start.9 = (bf16[256,1152]{1,0:T(8,128)(2,1)S(1)}, bf16[256,1152]{1,0:T(8,128)(2,1)}, u32[]{:S(2)}) copy-start(bf16[256,1152]{1,0:T(8,128)(2,1)} %copy-done.8) | copy-start | bytes 1769476
  39.3 20.2 %copy-start.3 = (s32[2]{0:T(128)S(1)}, s32[2]{0:T(128)}, u32[]{:S(2)}) copy-start(s32[2]{0:T(128)} %pad_add_fusion.at_ref) | copy-start | bytes 28
  39.3 90.5 %reduce-scatter.4.cloned.1.call-start = ((), (), s32[]{:S(2)}) async-start(), calls=%async_computation.3 | async-start | bytes 2621440 | tf_op jit(solution)/shard_map/reduce_scatter | solution.py:210
  48.0 125.1 %reduce-scatter.8.cloned.1.call-start = ((), (), s32[]{:S(2)}) async-start(), calls=%async_computation.5 | async-start | bytes 1179648 | tf_op jit(solution)/shard_map/reduce_scatter | solution.py:224
  48.1 8.9 %collective-permute-start.3 = (bf16[128,1152]{1,0:T(8,128)(2,1)S(1)}, bf16[128,1152]{1,0:T(8,128)(2,1)S(1)}, u32[]{:S(2)}, u32[]{:S(2)}) collective-permute-start(bf16[128,1152]{1,0:T(8,128)(2,1)S(1)} %slice.97), channel_id=1, source_target_pairs={{0,3},{1,0},{2,1},{3,2},{4,7},{5,4},{6,5},{7,6},{8,11},{9,8},{10,9... | collective-permute-start | bytes 884744 | tf_op jit(solution)/shard_map/ppermute | solution.py:22
  51.2 8.3 %collective-permute-start.4 = (bf16[128,1152]{1,0:T(8,128)(2,1)S(1)}, bf16[128,1152]{1,0:T(8,128)(2,1)S(1)}, u32[]{:S(2)}, u32[]{:S(2)}) collective-permute-start(bf16[128,1152]{1,0:T(8,128)(2,1)S(1)} %slice.98), channel_id=1, source_target_pairs={{0,1},{1,2},{2,3},{3,0},{4,5},{5,6},{6,7},{7,4},{8,9},{9,10},{10,1... | collective-permute-start | bytes 884744 | tf_op jit(solution)/shard_map/ppermute | solution.py:22
  59.5 2.2 %copy-start = (bf16[2,8,128,1024]{3,2,1,0:T(8,128)(2,1)S(1)}, bf16[2,8,128,1024]{3,2,1,0:T(8,128)(2,1)}, u32[]{:S(2)}) copy-start(bf16[2,8,128,1024]{3,2,1,0:T(8,128)(2,1)} %param.9) | copy-start | bytes 12582916
  72.2 52.7 %copy-start.1 = (f32[4,2,2,4,128,128]{5,4,3,2,1,0:T(8,128)}, f32[4,2,2,4,128,128]{5,4,3,2,1,0:T(8,128)S(1)}, u32[]{:S(2)}) copy-start(f32[4,2,2,4,128,128]{5,4,3,2,1,0:T(8,128)S(1)} %shard_map.58) | copy-start | bytes 12582916
  72.3 5.0 %collective-permute-start.5 = (f32[2,128,128]{2,1,0:T(8,128)S(1)}, f32[2,128,128]{2,1,0:T(8,128)S(1)}, u32[]{:S(2)}, u32[]{:S(2)}) collective-permute-start(f32[2,128,128]{2,1,0:T(8,128)S(1)} %get-tuple-element.16), channel_id=1, source_target_pairs={{0,16},{16,32},{32,48},{48,64},{64,80},{80,96},{96,112},{112,0},{1... | collective-permute-start | bytes 393224 | tf_op jit(solution)/shard_map/ppermute | solution.py:22
  77.3 8.4 %collective-permute-start.6 = (f32[4,128,128]{2,1,0:T(8,128)S(1)}, f32[4,128,128]{2,1,0:T(8,128)S(1)}, u32[]{:S(2)}, u32[]{:S(2)}) collective-permute-start(f32[4,128,128]{2,1,0:T(8,128)S(1)} %fusion.11), channel_id=1, source_target_pairs={{0,16},{16,32},{32,48},{48,64},{64,80},{80,96},{96,112},{112,0},{1... | collective-permute-start | bytes 786440 | tf_op jit(solution)/shard_map/ppermute | solution.py:22
  85.8 7.7 %collective-permute-start.7 = (f32[4,128,128]{2,1,0:T(8,128)S(1)}, f32[4,128,128]{2,1,0:T(8,128)S(1)}, u32[]{:S(2)}, u32[]{:S(2)}) collective-permute-start(f32[4,128,128]{2,1,0:T(8,128)S(1)} %fusion.12), channel_id=1, source_target_pairs={{0,16},{16,32},{32,48},{48,64},{64,80},{80,96},{96,112},{112,0},{1... | collective-permute-start | bytes 786440 | tf_op jit(solution)/shard_map/ppermute | solution.py:22
  86.4 6.3 %collective-permute-start.9 = (f32[2,128,128]{2,1,0:T(8,128)S(1)}, f32[2,128,128]{2,1,0:T(8,128)S(1)}, u32[]{:S(2)}, u32[]{:S(2)}) collective-permute-start(f32[2,128,128]{2,1,0:T(8,128)S(1)} %get-tuple-element.19), channel_id=1, source_target_pairs={{0,112},{16,0},{32,16},{48,32},{64,48},{80,64},{96,80},{112,96},{1... | collective-permute-start | bytes 393224 | tf_op jit(solution)/shard_map/ppermute | solution.py:22
  93.5 10.1 %collective-permute-start.10 = (f32[4,128,128]{2,1,0:T(8,128)S(1)}, f32[4,128,128]{2,1,0:T(8,128)S(1)}, u32[]{:S(2)}, u32[]{:S(2)}) collective-permute-start(f32[4,128,128]{2,1,0:T(8,128)S(1)} %get-tuple-element.15), channel_id=1, source_target_pairs={{0,112},{16,0},{32,16},{48,32},{64,48},{80,64},{96,80},{112,96},{1... | collective-permute-start | bytes 786440 | tf_op jit(solution)/shard_map/ppermute | solution.py:22
  103.7 10.7 %collective-permute-start.11 = (f32[4,128,128]{2,1,0:T(8,128)S(1)}, f32[4,128,128]{2,1,0:T(8,128)S(1)}, u32[]{:S(2)}, u32[]{:S(2)}) collective-permute-start(f32[4,128,128]{2,1,0:T(8,128)S(1)} %fusion.9), channel_id=1, source_target_pairs={{0,112},{16,0},{32,16},{48,32},{64,48},{80,64},{96,80},{112,96},{1... | collective-permute-start | bytes 786440 | tf_op jit(solution)/shard_map/ppermute | solution.py:22
  106.1 18.9 %collective-permute-start.8 = (f32[4,128,128]{2,1,0:T(8,128)S(1)}, f32[4,128,128]{2,1,0:T(8,128)S(1)}, u32[]{:S(2)}, u32[]{:S(2)}) collective-permute-start(f32[4,128,128]{2,1,0:T(8,128)S(1)} %get-tuple-element.14), channel_id=1, source_target_pairs={{0,16},{16,32},{32,48},{48,64},{64,80},{80,96},{96,112},{112,0},{1... | collective-permute-start | bytes 786440 | tf_op jit(solution)/shard_map/ppermute | solution.py:22
  114.5 10.5 %collective-permute-start.12 = (f32[4,128,128]{2,1,0:T(8,128)S(1)}, f32[4,128,128]{2,1,0:T(8,128)S(1)}, u32[]{:S(2)}, u32[]{:S(2)}) collective-permute-start(f32[4,128,128]{2,1,0:T(8,128)S(1)} %fusion.10), channel_id=1, source_target_pairs={{0,112},{16,0},{32,16},{48,32},{64,48},{80,64},{96,80},{112,96},{1... | collective-permute-start | bytes 786440 | tf_op jit(solution)/shard_map/ppermute | solution.py:22
  116.3 8.6 %collective-permute-start.17 = (f32[2,128,128]{2,1,0:T(8,128)S(1)}, f32[2,128,128]{2,1,0:T(8,128)S(1)}, u32[]{:S(2)}, u32[]{:S(2)}) collective-permute-start(f32[2,128,128]{2,1,0:T(8,128)S(1)} %get-tuple-element.17), channel_id=1, source_target_pairs={{0,112},{16,0},{32,16},{48,32},{64,48},{80,64},{96,80},{112,96},{1... | collective-permute-start | bytes 393224 | tf_op jit(solution)/shard_map/ppermute | solution.py:22
  119.9 5.0 %collective-permute-start.13 = (f32[2,128,128]{2,1,0:T(8,128)S(1)}, f32[2,128,128]{2,1,0:T(8,128)S(1)}, u32[]{:S(2)}, u32[]{:S(2)}) collective-permute-start(f32[2,128,128]{2,1,0:T(8,128)S(1)} %get-tuple-element.18), channel_id=1, source_target_pairs={{0,16},{16,32},{32,48},{48,64},{64,80},{80,96},{96,112},{112,0},{1... | collective-permute-start | bytes 393224 | tf_op jit(solution)/shard_map/ppermute | solution.py:22
  125.0 8.9 %collective-permute-start.14 = (f32[4,128,128]{2,1,0:T(8,128)S(1)}, f32[4,128,128]{2,1,0:T(8,128)S(1)}, u32[]{:S(2)}, u32[]{:S(2)}) collective-permute-start(f32[4,128,128]{2,1,0:T(8,128)S(1)} %get-tuple-element.13), channel_id=1, source_target_pairs={{0,16},{16,32},{32,48},{48,64},{64,80},{80,96},{96,112},{112,0},{1... | collective-permute-start | bytes 786440 | tf_op jit(solution)/shard_map/ppermute | solution.py:22
  129.8 10.6 %collective-permute-start.18 = (f32[4,128,128]{2,1,0:T(8,128)S(1)}, f32[4,128,128]{2,1,0:T(8,128)S(1)}, u32[]{:S(2)}, u32[]{:S(2)}) collective-permute-start(f32[4,128,128]{2,1,0:T(8,128)S(1)} %get-tuple-element.12), channel_id=1, source_target_pairs={{0,112},{16,0},{32,16},{48,32},{64,48},{80,64},{96,80},{112,96},{1... | collective-permute-start | bytes 786440 | tf_op jit(solution)/shard_map/ppermute | solution.py:22
  134.9 8.0 %collective-permute-start.15 = (f32[4,128,128]{2,1,0:T(8,128)S(1)}, f32[4,128,128]{2,1,0:T(8,128)S(1)}, u32[]{:S(2)}, u32[]{:S(2)}) collective-permute-start(f32[4,128,128]{2,1,0:T(8,128)S(1)} %fusion.4), channel_id=1, source_target_pairs={{0,16},{16,32},{32,48},{48,64},{64,80},{80,96},{96,112},{112,0},{1... | collective-permute-start | bytes 786440 | tf_op jit(solution)/shard_map/ppermute | solution.py:22
  144.0 9.4 %collective-permute-start.19 = (f32[4,128,128]{2,1,0:T(8,128)S(1)}, f32[4,128,128]{2,1,0:T(8,128)S(1)}, u32[]{:S(2)}, u32[]{:S(2)}) collective-permute-start(f32[4,128,128]{2,1,0:T(8,128)S(1)} %get-tuple-element.21), channel_id=1, source_target_pairs={{0,112},{16,0},{32,16},{48,32},{64,48},{80,64},{96,80},{112,96},{1... | collective-permute-start | bytes 786440 | tf_op jit(solution)/shard_map/ppermute | solution.py:22
  146.3 11.0 %collective-permute-start.16 = (f32[4,128,128]{2,1,0:T(8,128)S(1)}, f32[4,128,128]{2,1,0:T(8,128)S(1)}, u32[]{:S(2)}, u32[]{:S(2)}) collective-permute-start(f32[4,128,128]{2,1,0:T(8,128)S(1)} %get-tuple-element.20), channel_id=1, source_target_pairs={{0,16},{16,32},{32,48},{48,64},{64,80},{80,96},{96,112},{112,0},{1... | collective-permute-start | bytes 786440 | tf_op jit(solution)/shard_map/ppermute | solution.py:22
  154.3 7.9 %collective-permute-start.20 = (f32[4,128,128]{2,1,0:T(8,128)S(1)}, f32[4,128,128]{2,1,0:T(8,128)S(1)}, u32[]{:S(2)}, u32[]{:S(2)}) collective-permute-start(f32[4,128,128]{2,1,0:T(8,128)S(1)} %fusion.2), channel_id=1, source_target_pairs={{0,112},{16,0},{32,16},{48,32},{64,48},{80,64},{96,80},{112,96},{1... | collective-permute-start | bytes 786440 | tf_op jit(solution)/shard_map/ppermute | solution.py:22
  155.2 10.7 %collective-permute-start.21 = (f32[128,128]{1,0:T(8,128)S(1)}, f32[128,128]{1,0:T(8,128)S(1)}, u32[]{:S(2)}, u32[]{:S(2)}) collective-permute-start(f32[128,128]{1,0:T(8,128)S(1)} %slice_bitcast_fusion.19), channel_id=1, source_target_pairs={{0,4},{4,8},{8,12},{12,0},{1,5},{5,9},{9,13},{13,1},{2,6},{6,10},{... | collective-permute-start | bytes 196616 | tf_op jit(solution)/shard_map/ppermute | solution.py:22
  163.3 4.5 %collective-permute-start.23 = (f32[128,128]{1,0:T(8,128)S(1)}, f32[128,128]{1,0:T(8,128)S(1)}, u32[]{:S(2)}, u32[]{:S(2)}) collective-permute-start(f32[128,128]{1,0:T(8,128)S(1)} %slice_bitcast_fusion.18), channel_id=1, source_target_pairs={{0,12},{4,0},{8,4},{12,8},{1,13},{5,1},{9,5},{13,9},{2,14},{6,2},{... | collective-permute-start | bytes 196616 | tf_op jit(solution)/shard_map/ppermute | solution.py:22
  167.8 6.3 %collective-permute-start.24 = (f32[2,128,128]{2,1,0:T(8,128)S(1)}, f32[2,128,128]{2,1,0:T(8,128)S(1)}, u32[]{:S(2)}, u32[]{:S(2)}) collective-permute-start(f32[2,128,128]{2,1,0:T(8,128)S(1)} %get-tuple-element.23), channel_id=1, source_target_pairs={{0,12},{4,0},{8,4},{12,8},{1,13},{5,1},{9,5},{13,9},{2,14},{6,2},{... | collective-permute-start | bytes 393224 | tf_op jit(solution)/shard_map/ppermute | solution.py:22
  171.5 6.2 %collective-permute-start.22 = (f32[2,128,128]{2,1,0:T(8,128)S(1)}, f32[2,128,128]{2,1,0:T(8,128)S(1)}, u32[]{:S(2)}, u32[]{:S(2)}) collective-permute-start(f32[2,128,128]{2,1,0:T(8,128)S(1)} %get-tuple-element.22), channel_id=1, source_target_pairs={{0,4},{4,8},{8,12},{12,0},{1,5},{5,9},{9,13},{13,1},{2,6},{6,10},{... | collective-permute-start | bytes 393224 | tf_op jit(solution)/shard_map/ppermute | solution.py:22
  177.7 12.1 %collective-permute-start.26 = (bf16[2,128,128]{2,1,0:T(8,128)(2,1)S(1)}, bf16[2,128,128]{2,1,0:T(8,128)(2,1)S(1)}, u32[]{:S(2)}, u32[]{:S(2)}) collective-permute-start(bf16[2,128,128]{2,1,0:T(8,128)(2,1)S(1)} %broadcast_select_fusion), channel_id=1, source_target_pairs={{0,3},{16,19},{32,0},{48,16},{64,2},{80,18},{96,1},{112,17},{1,32}... | collective-permute-start | bytes 196616 | tf_op jit(solution)/shard_map/ppermute | solution.py:233
  186.6 11.0 %collective-permute-start.25 = (bf16[2,128,128]{2,1,0:T(8,128)(2,1)S(1)}, bf16[2,128,128]{2,1,0:T(8,128)(2,1)S(1)}, u32[]{:S(2)}, u32[]{:S(2)}) collective-permute-start(bf16[2,128,128]{2,1,0:T(8,128)(2,1)S(1)} %get-tuple-element.9), channel_id=1, source_target_pairs={{0,0},{16,16},{32,3},{48,19},{64,1},{80,17},{96,2},{112,18},{1,33}... | collective-permute-start | bytes 196616 | tf_op jit(solution)/shard_map/ppermute | solution.py:232
Sparse Core Ops, SparseCore 0:
  39.4 35.1 reduce-scatter.5
  77.3 31.9 reduce-scatter.3
  132.2 40.8 reduce-scatter.7

commit v3 on v2

v3 whole, which is shorter than its diff:
```python
import functools

import jax
import jax.numpy as jnp
from jax import lax
from jax.experimental import pallas as pl
from jax.experimental.pallas import tpu as pltpu
from jax.sharding import Mesh, PartitionSpec as P

PAIRS_DEV = 256
HALF = PAIRS_DEV // 2
DOMAIN = 8
LANES = 128
PACKED = (DOMAIN + 1) * LANES
FIRST = (0, 1)
SECOND = (3, 2)
MIB = 1024 * 1024


def shift(value, axis, step):
    size = lax.axis_size(axis)
    return lax.ppermute(value, axis, [(i, (i + step) % size) for i in range(size)])


def pack_kernel(base_ref, owner_in, tile_in, pair_in, a_in, o_ref, owner_ref, tile_ref, pair_ref, a_ref, sem):
    arriving = [
        pltpu.make_async_copy(source, target, sem.at[i])
        for i, (source, target) in enumerate(
            ((owner_in, owner_ref), (tile_in, tile_ref), (pair_in, pair_ref), (a_in, a_ref))
        )
    ]
    for copy in arriving:
        copy.start()
    for copy in arriving[:3]:
        copy.wait()
    rows = a_ref.shape[0]
    count = owner_ref.shape[0]
    tiles = tile_ref[...]
    slots = jnp.zeros((1, rows), jnp.int32)
    for t in range(count):
        slots = jnp.where(tiles == t, owner_ref[t], slots)
    slots = lax.rem(slots - base_ref[0] + count, count)
    pairs = pair_ref[...]
    in_pair = lax.broadcasted_iota(jnp.int32, (PAIRS_DEV, rows), 0) == pairs
    in_slot = lax.broadcasted_iota(jnp.int32, (count, rows), 0) == slots
    pair_hot = in_pair.astype(jnp.float32).astype(jnp.bfloat16)
    slot_hot = in_slot.astype(jnp.float32)
    slot_hot_narrow = slot_hot.astype(jnp.bfloat16)
    contract_rows = (((1,), (1,)), ((), ()))
    present = lax.dot_general(
        pair_hot, slot_hot_narrow, contract_rows, preferred_element_type=jnp.float32
    )
    present_t = lax.dot_general(
        slot_hot_narrow, pair_hot, contract_rows, preferred_element_type=jnp.float32
    )
    row_id = lax.broadcasted_iota(jnp.int32, (count, count), 0)
    col_id = lax.broadcasted_iota(jnp.int32, (count, count), 1)
    upper = (row_id < col_id).astype(jnp.float32).astype(jnp.bfloat16)
    lower = (row_id > col_id).astype(jnp.float32).astype(jnp.bfloat16)
    before = jnp.dot(present.astype(jnp.bfloat16), upper, preferred_element_type=jnp.float32)
    before_t = jnp.dot(lower, present_t.astype(jnp.bfloat16), preferred_element_type=jnp.float32)
    by_row = jnp.dot(
        before_t.astype(jnp.bfloat16), pair_hot, preferred_element_type=jnp.float32
    )
    rank = jnp.sum(by_row * slot_hot, axis=0, keepdims=True).astype(jnp.int32)
    slot_id = lax.broadcasted_iota(jnp.int32, (PAIRS_DEV, count), 1).astype(jnp.float32)
    lane = lax.broadcasted_iota(jnp.int32, (PAIRS_DEV, LANES), 1)
    table = jnp.zeros((PAIRS_DEV, LANES), jnp.float32)
    pair_id = lax.broadcasted_iota(jnp.int32, (PAIRS_DEV, rows), 0)
    arriving[3].wait()
    for i in range(DOMAIN):
        chosen = (pair_id == jnp.where(rank == i, pairs, -1)).astype(jnp.float32)
        o_ref[:, i * LANES : (i + 1) * LANES] = jnp.dot(
            chosen.astype(jnp.bfloat16), a_ref[...], preferred_element_type=jnp.float32
        ).astype(jnp.bfloat16)
        mine = jnp.where(before == i, present * slot_id, 0.0)
        table = jnp.where(lane == i, jnp.sum(mine, axis=1, keepdims=True), table)
    o_ref[:, DOMAIN * LANES :] = table.astype(jnp.bfloat16)


SMEM = pl.BlockSpec(memory_space=pltpu.SMEM)
VMEM = pl.BlockSpec(memory_space=pltpu.VMEM)
HBM = pl.BlockSpec(memory_space=pltpu.HBM)
ANY = pl.BlockSpec(memory_space=pl.ANY)
SMALL = pl.CostEstimate(flops=1024, bytes_accessed=1024, transcendentals=0)


def pinned(space, *arrays):
    return [pltpu.with_memory_space_constraint(array, space) for array in arrays]


def pack(amplitudes, tile_pairs, row_pairs, owner, base):
    rows = amplitudes.shape[0]
    return pl.pallas_call(
        pack_kernel,
        in_specs=[SMEM, HBM, HBM, HBM, HBM],
        out_specs=VMEM,
        out_shape=jax.ShapeDtypeStruct((PAIRS_DEV, PACKED), jnp.bfloat16),
        scratch_shapes=[
            pltpu.SMEM(owner.shape, jnp.int32),
            pltpu.VMEM((1, rows), jnp.int32),
            pltpu.VMEM((1, rows), jnp.int32),
            pltpu.VMEM(amplitudes.shape, jnp.bfloat16),
            pltpu.SemaphoreType.DMA((4,)),
        ],
        compiler_params=pltpu.CompilerParams(vmem_limit_bytes=32 * MIB),
        cost_estimate=SMALL,
    )(
        base,
        *pinned(
            pltpu.HBM, owner, tile_pairs.reshape(1, rows), row_pairs.reshape(1, rows), amplitudes
        ),
    )


def expand(piece, dense_ref, row):
    rows = piece.shape[0]
    count = dense_ref.shape[1] // LANES
    tiles = [piece[:, i * LANES : (i + 1) * LANES] for i in range(DOMAIN)]
    table = piece[:, DOMAIN * LANES :].astype(jnp.float32)
    slots = [jnp.broadcast_to(table[:, i : i + 1], (rows, LANES)) for i in range(DOMAIN)]
    for j in range(count):
        total = jnp.zeros((rows, LANES), jnp.bfloat16)
        for i in range(max(0, j - (count - DOMAIN)), min(DOMAIN - 1, j) + 1):
            mask = (slots[i] == j).astype(jnp.float32).astype(jnp.bfloat16)
            total = total + mask * tiles[i]
        dense_ref[row : row + rows, j * LANES : (j + 1) * LANES] = total


def multiply(piece_refs, blocks, dense_ref, acc_ref, done):
    own_in, other_in, own_ref, other_ref, sem = blocks
    arriving = {}
    for c in range(2):
        for zl in range(2):
            columns = pl.ds(zl * 512, 512)
            arriving[c, zl] = [
                pltpu.make_async_copy(
                    source.at[c, :, columns], target.at[c, :, columns], sem.at[i, c, zl]
                )
                for i, (source, target) in enumerate(((own_in, own_ref), (other_in, other_ref)))
            ]
            for copy in arriving[c, zl]:
                copy.start()
    row = 0
    for ref in piece_refs:
        for start in range(0, ref.shape[0], HALF):
            expand(ref[start : start + HALF, :], dense_ref, row)
            row += HALF
    depth = own_ref.shape[1]
    for c in range(2):
        for zl in range(2):
            columns = slice(zl * 512, (zl + 1) * 512)
            slot = 2 * c + zl
            for copy in arriving[c, zl]:
                copy.wait()
            acc_ref[slot] = jnp.dot(
                dense_ref[:, :depth], own_ref[c, :, columns], preferred_element_type=jnp.float32
            ) + jnp.dot(
                dense_ref[:, depth:], other_ref[c, :, columns], preferred_element_type=jnp.float32
            )
            done(c, zl, slot)


def first_kernel(*refs, block, taken):
    at_ref, piece_ref, own_in, other_in = refs[:4]
    o_ref, own_ref, other_ref, block_sem, dense_ref, acc_ref, sem = refs[4 + taken :]
    blocks = (own_in, other_in, own_ref, other_ref, block_sem)
    x = at_ref[0]
    copies = []

    def done(c, zl, slot):
        for half in range(2):
            for column in range(4):
                copies.append(
                    pltpu.make_async_copy(
                        acc_ref.at[slot, pl.ds(half * HALF, HALF), pl.ds(column * LANES, LANES)],
                        o_ref.at[4 * block + 2 * half + zl, lax.rem(column - x + 4, 4), c],
                        sem.at[slot, half, column],
                    )
                )
                copies[-1].start()

    multiply([piece_ref], blocks, dense_ref, acc_ref, done)
    for copy in copies:
        copy.wait()


def second_kernel(*refs, pieces):
    at_ref, piece_refs, refs = refs[0], refs[1 : 1 + pieces], refs[1 + pieces :]
    own_in, other_in, t0_ref, t1_ref, t2a_ref, t2b_ref, t3_ref, *refs = refs
    own_ref, other_ref, block_sem, dense_ref, acc_ref = refs
    blocks = (own_in, other_in, own_ref, other_ref, block_sem)
    x = at_ref[0]

    def done(c, zl, slot):
        for rel in range(4):
            column = pl.multiple_of(lax.rem(x + rel, 4) * LANES, LANES)
            for half in range(2):
                tile = acc_ref[slot, half * HALF : (half + 1) * HALF, pl.ds(column, LANES)]
                if rel == 2:
                    (t2a_ref, t2b_ref)[half][zl, c] = tile
                else:
                    (t0_ref, t1_ref, None, t3_ref)[rel][half, zl, c] = tile

    multiply(piece_refs, blocks, dense_ref, acc_ref, done)


def product_scratch(own):
    return [
        pltpu.VMEM(own.shape, own.dtype),
        pltpu.VMEM(own.shape, own.dtype),
        pltpu.SemaphoreType.DMA((2, 2, 2)),
        pltpu.VMEM((PAIRS_DEV, 2 * own.shape[1]), jnp.bfloat16),
        pltpu.VMEM((4, PAIRS_DEV, 512), jnp.float32),
    ]


def first_products(piece, own, other, at, block, earlier):
    taken = [] if earlier is None else [earlier]
    return pl.pallas_call(
        functools.partial(first_kernel, block=block, taken=len(taken)),
        in_specs=[SMEM, VMEM, HBM, HBM] + [HBM] * len(taken),
        out_specs=HBM,
        out_shape=pltpu.HBM((8, 4, 2, HALF, LANES), jnp.float32),
        scratch_shapes=product_scratch(own) + [pltpu.SemaphoreType.DMA((4, 2, 4))],
        input_output_aliases={4: 0} if taken else {},
        compiler_params=pltpu.CompilerParams(vmem_limit_bytes=24 * MIB),
        cost_estimate=SMALL
        if taken
        else pl.CostEstimate(flops=2**32, bytes_accessed=16 * MIB, transcendentals=0),
    )(at, piece, *pinned(pltpu.HBM, own, other, *taken))


def second_products(packed, own, other, at):
    whole = jax.ShapeDtypeStruct((2, 2, 2, HALF, LANES), jnp.float32)
    part = jax.ShapeDtypeStruct((2, 2, HALF, LANES), jnp.float32)
    return pl.pallas_call(
        functools.partial(second_kernel, pieces=len(packed)),
        in_specs=[SMEM] + [VMEM] * len(packed) + [HBM] * 2,
        out_specs=[VMEM] * 5,
        out_shape=[whole, whole, part, part, whole],
        scratch_shapes=product_scratch(own),
        compiler_params=pltpu.CompilerParams(vmem_limit_bytes=24 * MIB),
        cost_estimate=SMALL,
    )(at, *packed, *pinned(pltpu.HBM, own, other))


def step_kernel(near_ref, far_ref, up_ref, down_ref, up_out, down_out):
    up_out[...] = near_ref[...]
    down_out[...] = far_ref[...]
    up_out[0] += up_ref[...]
    down_out[1] += down_ref[...]


def x_step(near, far, up, down):
    return pl.pallas_call(
        step_kernel,
        in_specs=[VMEM] * 4,
        out_specs=[VMEM] * 2,
        out_shape=[jax.ShapeDtypeStruct(near.shape, jnp.float32)] * 2,
        compiler_params=pltpu.CompilerParams(vmem_limit_bytes=16 * MIB),
        cost_estimate=SMALL,
    )(near, far, up, down)


def turn_kernel(at_ref, *refs):
    z = at_ref[1]
    out_ref, up_ref, down_ref = refs[6:]
    for d in range(2):
        own_ref, left_ref, right_ref = refs[3 * d : 3 * d + 3]
        for half in range(2):
            for zl in range(2):
                away = lax.rem(4 * d + 2 * (1 - half) + zl - z + 8, 8)
                out_ref[away] = own_ref[half, zl] + left_ref[half, zl] + right_ref[half, zl]
    up_ref[...] = out_ref[4, 0]
    down_ref[...] = out_ref[4, 1]


def turn(at, parts):
    tile = jax.ShapeDtypeStruct((HALF, LANES), jnp.float32)
    return pl.pallas_call(
        turn_kernel,
        in_specs=[SMEM] + [VMEM] * 6,
        out_specs=[VMEM] * 3,
        out_shape=[jax.ShapeDtypeStruct((8, 2, HALF, LANES), jnp.float32), tile, tile],
        compiler_params=pltpu.CompilerParams(vmem_limit_bytes=16 * MIB),
        cost_estimate=SMALL,
    )(at, *parts)


def z_step_kernel(tiles_ref, up_ref, down_ref, up_out, down_out, *, near):
    far = 8 - near
    if near == 3:
        up_out[0] = tiles_ref[near, 0] + up_ref[...]
        up_out[1] = tiles_ref[near, 1]
        down_out[0] = tiles_ref[far, 0]
        down_out[1] = tiles_ref[far, 1] + down_ref[...]
    else:
        up_out[...] = tiles_ref[near] + up_ref[...]
        down_out[...] = tiles_ref[far] + down_ref[...]


def z_step(tiles, up, down, near):
    return pl.pallas_call(
        functools.partial(z_step_kernel, near=near),
        in_specs=[VMEM] * 3,
        out_specs=[VMEM] * 2,
        out_shape=[jax.ShapeDtypeStruct((2, HALF, LANES), jnp.float32)] * 2,
        compiler_params=pltpu.CompilerParams(vmem_limit_bytes=16 * MIB),
        cost_estimate=SMALL,
    )(tiles, up, down)


def split_kernel(tiles_ref, after_ref, *refs):
    out_refs, sem = refs[:-1], refs[-1]
    copies = [
        pltpu.make_async_copy(tiles_ref.at[i], out_refs[i], sem.at[i]) for i in range(len(out_refs))
    ]
    for copy in copies:
        copy.start()
    for copy in copies:
        copy.wait()


def split(tiles, after):
    return pl.pallas_call(
        split_kernel,
        in_specs=[HBM, ANY],
        out_specs=[VMEM] * 4,
        out_shape=[jax.ShapeDtypeStruct(tiles.shape[1:], jnp.float32)] * 4,
        scratch_shapes=[pltpu.SemaphoreType.DMA((4,))],
        compiler_params=pltpu.CompilerParams(vmem_limit_bytes=16 * MIB),
        cost_estimate=SMALL,
    )(*pinned(pltpu.HBM, tiles), after)


def placements():
    moves = ([], [])
    for y in range(4):
        for z in range(8):
            d, bit, zl = z // 4, (z % 4) // 2, z % 2
            first_target = ((2 * y + zl) * 4) + (y + FIRST[d]) % 4
            second_target = ((2 * y + zl) * 4) + (y + SECOND[d]) % 4
            moves[bit].append((z * 4 + y, first_target))
            moves[1 - bit].append((z * 4 + y, second_target))
    return moves


def body(amplitudes, tile_pairs, row_pairs, owner, integrals):
    pair, x, z = lax.axis_index("pair"), lax.axis_index("x"), lax.axis_index("z")
    slot_width = integrals.shape[1]
    own = integrals.reshape(integrals.shape[0], slot_width * amplitudes.shape[1], -1)
    other = shift(own, "pair", 1)

    base = (pair * slot_width).astype(jnp.int32).reshape(1)
    local = pack(amplitudes, tile_pairs, row_pairs, owner, base)
    after = shift(local, "slab", -1)
    before = shift(local, "slab", 1)
    after, before = lax.optimization_barrier((after, before))
    across = [shift(after[:HALF], "slab", -1), shift(before[HALF:], "slab", 1)]

    at = jnp.stack([x, z]).astype(jnp.int32)
    first = first_products(local, own, other, at, 0, None)
    first = first_products(after, own, other, at, 1, first)
    first = lax.psum_scatter(
        first.reshape(8, -1, LANES), "z", scatter_dimension=0, tiled=True
    ).reshape(4, 2, HALF, LANES)

    parts = []
    for packed in ([before], across):
        t0, t1, t2a, t2b, t3 = second_products(packed, own, other, at)
        up, down = x_step(t1, t3, shift(t2a, "x", 1), shift(t2b, "x", -1))
        parts += [t0, shift(up, "x", 1), shift(down, "x", -1)]
    tiles, up, down = turn(at, parts)
    token = None
    for near in (3, 2, 1):
        up, down = z_step(tiles, shift(up, "z", 1), shift(down, "z", -1), near)
        token = up if near == 2 else token
    second = tiles[0] + shift(up, "z", 1) + shift(down, "z", -1)

    r0, r1, r2, r3 = split(first, token)
    first = r0 + shift(r1, "x", 1) + shift(r3, "x", -1) + shift(r2, "x", 2)

    first = first.astype(jnp.bfloat16)
    second = second.astype(jnp.bfloat16)
    even = (z // 2) % 2 == 0
    moves = placements()
    top = lax.ppermute(jnp.where(even, first, second), ("z", "slab"), moves[0])
    bottom = lax.ppermute(jnp.where(even, second, first), ("z", "slab"), moves[1])
    return jnp.concatenate([top, bottom], axis=1).transpose(1, 0, 2)


def solution(mesh):
    fine = Mesh(mesh.devices.reshape(2, 8, 4, 4), ("pair", "z", "x", "slab"))
    return jax.shard_map(
        body,
        mesh=fine,
        in_specs=(
            P(("pair", "slab"), ("z", "x")),
            P(("pair", "slab")),
            P(("pair", "slab")),
            P(),
            P(None, "pair", ("z", "x"), "slab"),
        ),
        out_specs=P(("pair", "slab"), None, ("z", "x")),
        check_vma=False,
    )
```

time: 205 us -> 152 us (0.74)
  waiting for transfers between devices: 88.3 us -> 66.8 us
  starting transfers between devices: 57.3 us -> 40 us
  other arithmetic: 8.25 us -> 0.15 us
  local copies, waits for them, and re-layouts: 6.23 us -> 0.84 us
    ppermute x25 -> x24, waiting for transfers between devices: 77.5 us -> 57.8 us  [shift(): lax.ppermute(value, axis, [(i, (i + step) % size) for i in range(size)])]
    ppermute x25 -> x24, starting transfers between devices: 46.4 us -> 31.2 us  [shift(): lax.ppermute(value, axis, [(i, (i + step) % size) for i in range(size)])]
    unnamed x20 -> x0, local copies, waits for them, and re-layouts: 5.34 us -> none
    add x11 -> x0, other arithmetic: 4.42 us -> none  [the longest x2 1.17 us: sum_over_z(): up = shift(tiles(1) + up, 'z', 1)]
    concatenate x1 -> x0, other arithmetic: 2.27 us -> none  [body(): jnp.concatenate(firsts)]
    ppermute x1, starting transfers between devices: 8.88 us -> 6.82 us  [body(): lax.ppermute(jnp.where(even, second, first), ('z', 'slab'), moves[1])]
    pallas_call x4 -> x12, Pallas kernels: 31.5 us -> 30.1 us  [the longest x2 12.3 us: first_products(): pl.pallas_call(functools.partial(first_kernel, block=block, taken=len(tak...]
  transfers between devices with their start and end apart: 30 -> 27, of which waited for: 21 -> 16; matrix products, arithmetic and copies ran while one was open for 4% -> 0% of each run, Pallas kernels for 11% -> 12%
where the time goes in v3:
time: 152 us; the launch traced here: 151 us
  waiting for transfers between devices  66.8 us (44%)
  starting transfers between devices  40 us (26%)
  Pallas kernels  30.1 us (20%)
  between operations  13.5 us (9%)
    ppermute x24, waiting for transfers between devices, shift(): lax.ppermute(value, axis, [(i, (i + step) % size) for i in range(size)])  57.8 us
    ppermute x24, starting transfers between devices, shift(): lax.ppermute(value, axis, [(i, (i + step) % size) for i in range(size)])  31.2 us
    pallas_call x2, Pallas kernels, first_products(): pl.pallas_call(functools.partial(first_kernel, block=block, taken=len(tak...  12.3 us
    pallas_call x2, Pallas kernels, second_products(): pl.pallas_call(functools.partial(second_kernel, pieces=len(packed)), in_s...  11.5 us
    ppermute x1, waiting for transfers between devices, body(): top = lax.ppermute(jnp.where(even, first, second), ('z', 'slab'), moves[0])  8.26 us
    ppermute x1, starting transfers between devices, body(): lax.ppermute(jnp.where(even, second, first), ('z', 'slab'), moves[1])  6.82 us
    pallas_call x1, Pallas kernels, pack(): pl.pallas_call(pack_kernel, in_specs=[SMEM, HBM, HBM, HBM, HBM], out_spec...  4.19 us
  transfers between devices with their start and end apart: 27, of which 16 were waited for; matrix products, arithmetic and copies ran while one was open for 0% of the time, Pallas kernels for 12%

profile of v3, /device:TPU:40, one launch (start us, length us, event | category | flops | bytes accessed | tf_op | source)
XLA Modules:
  0.0 151.4 jit_solution(11273471426874337496)
XLA Ops:
  6.5 4.2 %shard_map.55.refs_1_ = bf16[256,1152]{1,0:T(8,128)(2,1)S(1)} custom-call(s32[1]{0:T(128)} %bitcast.2.base_ref, s32[16]{0:T(128)} %owner_in.1, s32[1,2048]{1,0:T(1,128)} %bitcast.24, s32[1,2048]{1,0:T(1,128)} %bitcast.25, bf16[2048,128]{1,0:T(8,128)(2,1)} %a_in.1), custom_call_target="tpu_custom_call" | custom-call | flops 1024 | bytes 1024 | tf_op jit(solution)/shard_map/pallas_call | solution.py:94
  10.7 0.5 collective-permute-start
  11.3 1.6 %collective-permute-start.1 = (bf16[256,1152]{1,0:T(8,128)(2,1)S(1)}, bf16[256,1152]{1,0:T(8,128)(2,1)S(1)}, u32[]{:S(2)}, u32[]{:S(2)}) collective-permute-start(bf16[256,1152]{1,0:T(8,128)(2,1)S(1)} %shard_map.55.refs_1_), channel_id=1, source_target_pairs={{0,1},{1,2},{2,3},{3,0},{4,5},{5,6},{6,7},{7,4},{8,9},{9,10},{10,1... | collective-permute-start | bytes 1769480 | tf_op jit(solution)/shard_map/ppermute | solution.py:22
  12.9 13.6 %collective-permute-done.refs_1_ = bf16[256,1152]{1,0:T(8,128)(2,1)S(1)} collective-permute-done((bf16[256,1152]{1,0:T(8,128)(2,1)S(1)}, bf16[256,1152]{1,0:T(8,128)(2,1)S(1)}, u32[]{:S(2)}, u32[]{:S(2)}) %collective-permute-start) | collective-permute-done | bytes 589856 | tf_op jit(solution)/shard_map/ppermute | solution.py:22
  26.6 1.4 collective-permute-done.1.refs_1_
  28.0 6.1 %shard_map.56.refs_4_ = f32[8,4,2,128,128]{4,3,2,1,0:T(8,128)} custom-call(s32[2]{0:T(128)S(1)} %pad_add_fusion.refs_0_.at_ref, bf16[256,1152]{1,0:T(8,128)(2,1)S(1)} %shard_map.55.refs_1_, bf16[2,1024,1024]{2,1,0:T(8,128)(2,1)} %bitcast.18, bf16[2,1024,1024]{2,1,0:T(8,128)(2,1)} %collective-permute-done.2.refs_3_.refs_4_), custom_call_target="tpu_custom_call" | custom-call | flops 4294967296 | bytes 16777216 | tf_op jit(solution)/shard_map/pallas_call | solution.py:220
  34.1 6.1 %shard_map.57 = f32[8,4,2,128,128]{4,3,2,1,0:T(8,128)} custom-call(s32[2]{0:T(128)S(1)} %pad_add_fusion.refs_0_.at_ref, bf16[256,1152]{1,0:T(8,128)(2,1)S(1)} %collective-permute-done.refs_1_, bf16[2,1024,1024]{2,1,0:T(8,128)(2,1)} %bitcast.19, bf16[2,1024,1024]{2,1,0:T(8,128)(2,1)} %collective-permute-done.2.refs_3_.refs_4_, ...), custom_call_target="tpu_custom_call", output_to_operand_aliasing={{}: (4, {})} | custom-call | flops 1024 | bytes 1024 | tf_op jit(solution)/shard_map/pallas_call | solution.py:220
  40.3 3.2 %collective-permute-start.7 = (bf16[128,1152]{1,0:T(8,128)(2,1)S(1)}, bf16[128,1152]{1,0:T(8,128)(2,1)S(1)}, u32[]{:S(2)}, u32[]{:S(2)}) collective-permute-start(bf16[128,1152]{1,0:T(8,128)(2,1)S(1)} %slice.9), channel_id=1, source_target_pairs={{0,3},{1,0},{2,1},{3,2},{4,7},{5,4},{6,5},{7,6},{8,11},{9,8},{10,9... | collective-permute-start | bytes 884744 | tf_op jit(solution)/shard_map/ppermute | solution.py:22
  43.6 0.1 collective-permute-start.8
  43.7 5.3 %shard_map.58 = (f32[2,2,2,128,128]{4,3,2,1,0:T(8,128)S(1)}, f32[2,2,2,128,128]{4,3,2,1,0:T(8,128)S(1)}, f32[2,2,128,128]{3,2,1,0:T(8,128)S(1)}, f32[2,2,128,128...) custom-call(s32[2]{0:T(128)S(1)} %pad_add_fusion.refs_0_.at_ref, bf16[256,1152]{1,0:T(8,128)(2,1)S(1)} %collective-permute-done.1.refs_1_, ...), custom_call_target="tpu_custom_call" | custom-call | flops 1024 | bytes 1024 | tf_op jit(solution)/shard_map/pallas_call | solution.py:237
  49.0 1.6 %collective-permute-start.3 = (f32[2,2,128,128]{3,2,1,0:T(8,128)S(1)}, f32[2,2,128,128]{3,2,1,0:T(8,128)S(1)}, u32[]{:S(2)}, u32[]{:S(2)}) collective-permute-start(f32[2,2,128,128]{3,2,1,0:T(8,128)S(1)} %get-tuple-element.39), channel_id=1, source_target_pairs={{0,4},{4,8},{8,12},{12,0},{1,5},{5,9},{9,13},{13,1},{2,6},{6,10},{... | collective-permute-start | bytes 786440 | tf_op jit(solution)/shard_map/ppermute | solution.py:22
  50.6 1.8 %collective-permute-start.4 = (f32[2,2,128,128]{3,2,1,0:T(8,128)S(1)}, f32[2,2,128,128]{3,2,1,0:T(8,128)S(1)}, u32[]{:S(2)}, u32[]{:S(2)}) collective-permute-start(f32[2,2,128,128]{3,2,1,0:T(8,128)S(1)} %get-tuple-element.40), channel_id=1, source_target_pairs={{0,12},{4,0},{8,4},{12,8},{1,13},{5,1},{9,5},{13,9},{2,14},{6,2},{... | collective-permute-start | bytes 786440 | tf_op jit(solution)/shard_map/ppermute | solution.py:22
  52.3 6.2 %shard_map.60 = (f32[2,2,2,128,128]{4,3,2,1,0:T(8,128)S(1)}, f32[2,2,2,128,128]{4,3,2,1,0:T(8,128)S(1)}, f32[2,2,128,128]{3,2,1,0:T(8,128)S(1)}, f32[2,2,128,128...) custom-call(s32[2]{0:T(128)S(1)} %pad_add_fusion.refs_0_.at_ref, bf16[128,1152]{1,0:T(8,128)(2,1)S(1)} %collective-permute-done.7.refs_1_, ...), custom_call_target="tpu_custom_call" | custom-call | flops 1024 | bytes 1024 | tf_op jit(solution)/shard_map/pallas_call | solution.py:237
  58.5 1.0 collective-permute-start.9
  59.5 2.3 %collective-permute-start.10 = (f32[2,2,128,128]{3,2,1,0:T(8,128)S(1)}, f32[2,2,128,128]{3,2,1,0:T(8,128)S(1)}, u32[]{:S(2)}, u32[]{:S(2)}) collective-permute-start(f32[2,2,128,128]{3,2,1,0:T(8,128)S(1)} %get-tuple-element.47), channel_id=1, source_target_pairs={{0,12},{4,0},{8,4},{12,8},{1,13},{5,1},{9,5},{13,9},{2,14},{6,2},{... | collective-permute-start | bytes 786440 | tf_op jit(solution)/shard_map/ppermute | solution.py:22
  61.9 0.1 shard_map.59
  61.9 0.1 collective-permute-start.5
  62.0 3.2 %collective-permute-start.6 = (f32[2,2,2,128,128]{4,3,2,1,0:T(8,128)S(1)}, f32[2,2,2,128,128]{4,3,2,1,0:T(8,128)S(1)}, u32[]{:S(2)}, u32[]{:S(2)}) collective-permute-start(f32[2,2,2,128,128]{4,3,2,1,0:T(8,128)S(1)} %get-tuple-element.42), channel_id=1, source_target_pairs={{0,12},{4,0},{8,4},{12,8},{1,13},{5,1},{9,5},{13,9},{2,14},{6,2},{... | collective-permute-start | bytes 1572872 | tf_op jit(solution)/shard_map/ppermute | solution.py:22
  65.3 3.8 %collective-permute-done.9.up_ref = f32[2,2,128,128]{3,2,1,0:T(8,128)S(1)} collective-permute-done((f32[2,2,128,128]{3,2,1,0:T(8,128)S(1)}, f32[2,2,128,128]{3,2,1,0:T(8,128)S(1)}, u32[]{:S(2)}, u32[]{:S(2)}) %collective-permute-start.9) | collective-permute-done | bytes 262176 | tf_op jit(solution)/shard_map/ppermute | solution.py:22
  69.1 0.1 shard_map.61
  69.2 1.2 collective-permute-start.11
  70.4 2.1 %collective-permute-start.12 = (f32[2,2,2,128,128]{4,3,2,1,0:T(8,128)S(1)}, f32[2,2,2,128,128]{4,3,2,1,0:T(8,128)S(1)}, u32[]{:S(2)}, u32[]{:S(2)}) collective-permute-start(f32[2,2,2,128,128]{4,3,2,1,0:T(8,128)S(1)} %get-tuple-element.49), channel_id=1, source_target_pairs={{0,12},{4,0},{8,4},{12,8},{1,13},{5,1},{9,5},{13,9},{2,14},{6,2},{... | collective-permute-start | bytes 1572872 | tf_op jit(solution)/shard_map/ppermute | solution.py:22
  72.5 7.8 %collective-permute-done.5.refs_1_ = f32[2,2,2,128,128]{4,3,2,1,0:T(8,128)S(1)} collective-permute-done((f32[2,2,2,128,128]{4,3,2,1,0:T(8,128)S(1)}, f32[2,2,2,128,128]{4,3,2,1,0:T(8,128)S(1)}, u32[]{:S(2)}, u32[]{:S(2)}) %collective-permute-start.5) | collective-permute-done | bytes 524320 | tf_op jit(solution)/shard_map/ppermute | solution.py:22
  80.3 8.6 %collective-permute-done.11.refs_4_ = f32[2,2,2,128,128]{4,3,2,1,0:T(8,128)S(1)} collective-permute-done((f32[2,2,2,128,128]{4,3,2,1,0:T(8,128)S(1)}, f32[2,2,2,128,128]{4,3,2,1,0:T(8,128)S(1)}, u32[]{:S(2)}, u32[]{:S(2)}) %collective-permute-start.11) | collective-permute-done | bytes 524320 | tf_op jit(solution)/shard_map/ppermute | solution.py:22
  88.9 0.7 shard_map.62
  89.7 2.0 %collective-permute-start.13 = (f32[128,128]{1,0:T(8,128)S(1)}, f32[128,128]{1,0:T(8,128)S(1)}, u32[]{:S(2)}, u32[]{:S(2)}) collective-permute-start(f32[128,128]{1,0:T(8,128)S(1)} %get-tuple-element.51), channel_id=1, source_target_pairs={{0,16},{16,32},{32,48},{48,64},{64,80},{80,96},{96,112},{112,0},{1... | collective-permute-start | bytes 196616 | tf_op jit(solution)/shard_map/ppermute | solution.py:22
  91.8 3.7 %collective-permute-done.13.up_ref = f32[128,128]{1,0:T(8,128)S(1)} collective-permute-done((f32[128,128]{1,0:T(8,128)S(1)}, f32[128,128]{1,0:T(8,128)S(1)}, u32[]{:S(2)}, u32[]{:S(2)}) %collective-permute-start.13) | collective-permute-done | bytes 65568 | tf_op jit(solution)/shard_map/ppermute | solution.py:22
  95.5 1.2 collective-permute-done.14.down_ref
  96.7 2.5 %collective-permute-start.15 = (f32[2,128,128]{2,1,0:T(8,128)S(1)}, f32[2,128,128]{2,1,0:T(8,128)S(1)}, u32[]{:S(2)}, u32[]{:S(2)}) collective-permute-start(f32[2,128,128]{2,1,0:T(8,128)S(1)} %get-tuple-element.53), channel_id=1, source_target_pairs={{0,16},{16,32},{32,48},{48,64},{64,80},{80,96},{96,112},{112,0},{1... | collective-permute-start | bytes 393224 | tf_op jit(solution)/shard_map/ppermute | solution.py:22
  99.2 2.7 %collective-permute-done.15.up_ref = f32[2,128,128]{2,1,0:T(8,128)S(1)} collective-permute-done((f32[2,128,128]{2,1,0:T(8,128)S(1)}, f32[2,128,128]{2,1,0:T(8,128)S(1)}, u32[]{:S(2)}, u32[]{:S(2)}) %collective-permute-start.15) | collective-permute-done | bytes 131104 | tf_op jit(solution)/shard_map/ppermute | solution.py:22
  102.0 3.5 %collective-permute-done.16.down_ref = f32[2,128,128]{2,1,0:T(8,128)S(1)} collective-permute-done((f32[2,128,128]{2,1,0:T(8,128)S(1)}, f32[2,128,128]{2,1,0:T(8,128)S(1)}, u32[]{:S(2)}, u32[]{:S(2)}) %collective-permute-start.16) | collective-permute-done | bytes 131104 | tf_op jit(solution)/shard_map/ppermute | solution.py:22
  105.5 2.1 %collective-permute-start.20 = (f32[2,128,128]{2,1,0:T(8,128)S(1)}, f32[2,128,128]{2,1,0:T(8,128)S(1)}, u32[]{:S(2)}, u32[]{:S(2)}) collective-permute-start(f32[2,128,128]{2,1,0:T(8,128)S(1)} %get-tuple-element.55.after_ref), channel_id=1, source_target_pairs={{0,16},{16,32},{32,48},{48,64},{64,80},{80,96},{96,112},{112,0},{1... | collective-permute-start | bytes 393224 | tf_op jit(solution)/shard_map/ppermute | solution.py:22
  107.6 2.9 %collective-permute-done.20.up_ref = f32[2,128,128]{2,1,0:T(8,128)S(1)} collective-permute-done((f32[2,128,128]{2,1,0:T(8,128)S(1)}, f32[2,128,128]{2,1,0:T(8,128)S(1)}, u32[]{:S(2)}, u32[]{:S(2)}) %collective-permute-start.20) | collective-permute-done | bytes 131104 | tf_op jit(solution)/shard_map/ppermute | solution.py:22
  110.5 3.0 %collective-permute-done.21.down_ref = f32[2,128,128]{2,1,0:T(8,128)S(1)} collective-permute-done((f32[2,128,128]{2,1,0:T(8,128)S(1)}, f32[2,128,128]{2,1,0:T(8,128)S(1)}, u32[]{:S(2)}, u32[]{:S(2)}) %collective-permute-start.21) | collective-permute-done | bytes 131104 | tf_op jit(solution)/shard_map/ppermute | solution.py:22
  113.5 0.4 collective-permute-start.23
  113.9 1.7 %collective-permute-start.22 = (f32[2,128,128]{2,1,0:T(8,128)S(1)}, f32[2,128,128]{2,1,0:T(8,128)S(1)}, u32[]{:S(2)}, u32[]{:S(2)}) collective-permute-start(f32[2,128,128]{2,1,0:T(8,128)S(1)} %get-tuple-element.61), channel_id=1, source_target_pairs={{0,16},{16,32},{32,48},{48,64},{64,80},{80,96},{96,112},{112,0},{1... | collective-permute-start | bytes 393224 | tf_op jit(solution)/shard_map/ppermute | solution.py:22
  115.6 1.1 shard_map.65
  116.8 1.2 collective-permute-start.19
  118.0 1.7 %collective-permute-start.18 = (f32[2,128,128]{2,1,0:T(8,128)S(1)}, f32[2,128,128]{2,1,0:T(8,128)S(1)}, u32[]{:S(2)}, u32[]{:S(2)}) collective-permute-start(f32[2,128,128]{2,1,0:T(8,128)S(1)} %get-tuple-element.58), channel_id=1, source_target_pairs={{0,12},{4,0},{8,4},{12,8},{1,13},{5,1},{9,5},{13,9},{2,14},{6,2},{... | collective-permute-start | bytes 393224 | tf_op jit(solution)/shard_map/ppermute | solution.py:22
  119.7 0.8 collective-permute-start.17
  120.5 2.8 %collective-permute-done.19 = f32[2,128,128]{2,1,0:T(8,128)S(1)} collective-permute-done((f32[2,128,128]{2,1,0:T(8,128)S(1)}, f32[2,128,128]{2,1,0:T(8,128)S(1)}, u32[]{:S(2)}, u32[]{:S(2)}) %collective-permute-start.19) | collective-permute-done | bytes 131104 | tf_op jit(solution)/shard_map/ppermute | solution.py:22
  123.3 1.6 %collective-permute-done.18 = f32[2,128,128]{2,1,0:T(8,128)S(1)} collective-permute-done((f32[2,128,128]{2,1,0:T(8,128)S(1)}, f32[2,128,128]{2,1,0:T(8,128)S(1)}, u32[]{:S(2)}, u32[]{:S(2)}) %collective-permute-start.18) | collective-permute-done | bytes 131104 | tf_op jit(solution)/shard_map/ppermute | solution.py:22
  124.9 1.0 collective-permute-done.17
  126.0 6.8 %collective-permute-start.25 = (bf16[2,128,128]{2,1,0:T(8,128)(2,1)S(1)}, bf16[2,128,128]{2,1,0:T(8,128)(2,1)S(1)}, u32[]{:S(2)}, u32[]{:S(2)}) collective-permute-start(bf16[2,128,128]{2,1,0:T(8,128)(2,1)S(1)} %broadcast_select_fusion), channel_id=1, source_target_pairs={{0,3},{16,19},{32,0},{48,16},{64,2},{80,18},{96,1},{112,17},{1,32}... | collective-permute-start | bytes 196616 | tf_op jit(solution)/shard_map/ppermute | solution.py:389
  132.8 1.9 %collective-permute-start.24 = (bf16[2,128,128]{2,1,0:T(8,128)(2,1)S(1)}, bf16[2,128,128]{2,1,0:T(8,128)(2,1)S(1)}, u32[]{:S(2)}, u32[]{:S(2)}) collective-permute-start(bf16[2,128,128]{2,1,0:T(8,128)(2,1)S(1)} %get-tuple-element.63), channel_id=1, source_target_pairs={{0,0},{16,16},{32,3},{48,19},{64,1},{80,17},{96,2},{112,18},{1,33}... | collective-permute-start | bytes 196616 | tf_op jit(solution)/shard_map/ppermute | solution.py:388
  134.7 0.8 collective-permute-done.25
  135.5 8.3 %collective-permute-done.24 = bf16[2,128,128]{2,1,0:T(8,128)(2,1)S(1)} collective-permute-done((bf16[2,128,128]{2,1,0:T(8,128)(2,1)S(1)}, bf16[2,128,128]{2,1,0:T(8,128)(2,1)S(1)}, u32[]{:S(2)}, u32[]{:S(2)}) %collective-permute-start.24) | collective-permute-done | bytes 65568 | tf_op jit(solution)/shard_map/ppermute | solution.py:388
  143.8 0.8 copy.7
  (26 shorter events, 0.4 us)
Async XLA Ops:
  6.5 109.1 %reduce-scatter.2.cloned.1.call-start = ((), (), s32[]{:S(2)}) async-start(), calls=%async_computation.1 | async-start | bytes 4718592 | tf_op jit(solution)/shard_map/reduce_scatter | solution.py:365
  6.5 21.5 %collective-permute-start.2 = (bf16[2,1024,1024]{2,1,0:T(8,128)(2,1)}, bf16[2,1024,1024]{2,1,0:T(8,128)(2,1)}, u32[]{:S(2)}, u32[]{:S(2)}) collective-permute-start(bf16[2,1024,1024]{2,1,0:T(8,128)(2,1)} %bitcast.17), channel_id=1, source_target_pairs={{0,128},{128,0},{1,129},{129,1},{2,130},{130,2},{3,131},{131,3},{4... | collective-permute-start | bytes 12582920 | tf_op jit(solution)/shard_map/ppermute | solution.py:22
  10.7 15.8 %collective-permute-start = (bf16[256,1152]{1,0:T(8,128)(2,1)S(1)}, bf16[256,1152]{1,0:T(8,128)(2,1)S(1)}, u32[]{:S(2)}, u32[]{:S(2)}) collective-permute-start(bf16[256,1152]{1,0:T(8,128)(2,1)S(1)} %shard_map.55.refs_1_), channel_id=1, source_target_pairs={{0,3},{1,0},{2,1},{3,2},{4,7},{5,4},{6,5},{7,6},{8,11},{9,8},{10,9... | collective-permute-start | bytes 1769480 | tf_op jit(solution)/shard_map/ppermute | solution.py:22
  11.3 16.7 %collective-permute-start.1 = (bf16[256,1152]{1,0:T(8,128)(2,1)S(1)}, bf16[256,1152]{1,0:T(8,128)(2,1)S(1)}, u32[]{:S(2)}, u32[]{:S(2)}) collective-permute-start(bf16[256,1152]{1,0:T(8,128)(2,1)S(1)} %shard_map.55.refs_1_), channel_id=1, source_target_pairs={{0,1},{1,2},{2,3},{3,0},{4,5},{5,6},{6,7},{7,4},{8,9},{9,10},{10,1... | collective-permute-start | bytes 1769480 | tf_op jit(solution)/shard_map/ppermute | solution.py:22
  40.3 12.0 %collective-permute-start.7 = (bf16[128,1152]{1,0:T(8,128)(2,1)S(1)}, bf16[128,1152]{1,0:T(8,128)(2,1)S(1)}, u32[]{:S(2)}, u32[]{:S(2)}) collective-permute-start(bf16[128,1152]{1,0:T(8,128)(2,1)S(1)} %slice.9), channel_id=1, source_target_pairs={{0,3},{1,0},{2,1},{3,2},{4,7},{5,4},{6,5},{7,6},{8,11},{9,8},{10,9... | collective-permute-start | bytes 884744 | tf_op jit(solution)/shard_map/ppermute | solution.py:22
  43.6 8.8 %collective-permute-start.8 = (bf16[128,1152]{1,0:T(8,128)(2,1)S(1)}, bf16[128,1152]{1,0:T(8,128)(2,1)S(1)}, u32[]{:S(2)}, u32[]{:S(2)}) collective-permute-start(bf16[128,1152]{1,0:T(8,128)(2,1)S(1)} %slice.10), channel_id=1, source_target_pairs={{0,1},{1,2},{2,3},{3,0},{4,5},{5,6},{6,7},{7,4},{8,9},{9,10},{10,1... | collective-permute-start | bytes 884744 | tf_op jit(solution)/shard_map/ppermute | solution.py:22
  49.0 12.8 %collective-permute-start.3 = (f32[2,2,128,128]{3,2,1,0:T(8,128)S(1)}, f32[2,2,128,128]{3,2,1,0:T(8,128)S(1)}, u32[]{:S(2)}, u32[]{:S(2)}) collective-permute-start(f32[2,2,128,128]{3,2,1,0:T(8,128)S(1)} %get-tuple-element.39), channel_id=1, source_target_pairs={{0,4},{4,8},{8,12},{12,0},{1,5},{5,9},{9,13},{13,1},{2,6},{6,10},{... | collective-permute-start | bytes 786440 | tf_op jit(solution)/shard_map/ppermute | solution.py:22
  50.6 11.3 %collective-permute-start.4 = (f32[2,2,128,128]{3,2,1,0:T(8,128)S(1)}, f32[2,2,128,128]{3,2,1,0:T(8,128)S(1)}, u32[]{:S(2)}, u32[]{:S(2)}) collective-permute-start(f32[2,2,128,128]{3,2,1,0:T(8,128)S(1)} %get-tuple-element.40), channel_id=1, source_target_pairs={{0,12},{4,0},{8,4},{12,8},{1,13},{5,1},{9,5},{13,9},{2,14},{6,2},{... | collective-permute-start | bytes 786440 | tf_op jit(solution)/shard_map/ppermute | solution.py:22
  58.5 10.5 %collective-permute-start.9 = (f32[2,2,128,128]{3,2,1,0:T(8,128)S(1)}, f32[2,2,128,128]{3,2,1,0:T(8,128)S(1)}, u32[]{:S(2)}, u32[]{:S(2)}) collective-permute-start(f32[2,2,128,128]{3,2,1,0:T(8,128)S(1)} %get-tuple-element.46), channel_id=1, source_target_pairs={{0,4},{4,8},{8,12},{12,0},{1,5},{5,9},{9,13},{13,1},{2,6},{6,10},{... | collective-permute-start | bytes 786440 | tf_op jit(solution)/shard_map/ppermute | solution.py:22
  59.5 9.5 %collective-permute-start.10 = (f32[2,2,128,128]{3,2,1,0:T(8,128)S(1)}, f32[2,2,128,128]{3,2,1,0:T(8,128)S(1)}, u32[]{:S(2)}, u32[]{:S(2)}) collective-permute-start(f32[2,2,128,128]{3,2,1,0:T(8,128)S(1)} %get-tuple-element.47), channel_id=1, source_target_pairs={{0,12},{4,0},{8,4},{12,8},{1,13},{5,1},{9,5},{13,9},{2,14},{6,2},{... | collective-permute-start | bytes 786440 | tf_op jit(solution)/shard_map/ppermute | solution.py:22
  61.9 18.4 %collective-permute-start.5 = (f32[2,2,2,128,128]{4,3,2,1,0:T(8,128)S(1)}, f32[2,2,2,128,128]{4,3,2,1,0:T(8,128)S(1)}, u32[]{:S(2)}, u32[]{:S(2)}) collective-permute-start(f32[2,2,2,128,128]{4,3,2,1,0:T(8,128)S(1)} %get-tuple-element.41), channel_id=1, source_target_pairs={{0,4},{4,8},{8,12},{12,0},{1,5},{5,9},{9,13},{13,1},{2,6},{6,10},{... | collective-permute-start | bytes 1572872 | tf_op jit(solution)/shard_map/ppermute | solution.py:22
  62.0 18.3 %collective-permute-start.6 = (f32[2,2,2,128,128]{4,3,2,1,0:T(8,128)S(1)}, f32[2,2,2,128,128]{4,3,2,1,0:T(8,128)S(1)}, u32[]{:S(2)}, u32[]{:S(2)}) collective-permute-start(f32[2,2,2,128,128]{4,3,2,1,0:T(8,128)S(1)} %get-tuple-element.42), channel_id=1, source_target_pairs={{0,12},{4,0},{8,4},{12,8},{1,13},{5,1},{9,5},{13,9},{2,14},{6,2},{... | collective-permute-start | bytes 1572872 | tf_op jit(solution)/shard_map/ppermute | solution.py:22
  69.2 19.8 %collective-permute-start.11 = (f32[2,2,2,128,128]{4,3,2,1,0:T(8,128)S(1)}, f32[2,2,2,128,128]{4,3,2,1,0:T(8,128)S(1)}, u32[]{:S(2)}, u32[]{:S(2)}) collective-permute-start(f32[2,2,2,128,128]{4,3,2,1,0:T(8,128)S(1)} %get-tuple-element.48), channel_id=1, source_target_pairs={{0,4},{4,8},{8,12},{12,0},{1,5},{5,9},{9,13},{13,1},{2,6},{6,10},{... | collective-permute-start | bytes 1572872 | tf_op jit(solution)/shard_map/ppermute | solution.py:22
  70.4 18.5 %collective-permute-start.12 = (f32[2,2,2,128,128]{4,3,2,1,0:T(8,128)S(1)}, f32[2,2,2,128,128]{4,3,2,1,0:T(8,128)S(1)}, u32[]{:S(2)}, u32[]{:S(2)}) collective-permute-start(f32[2,2,2,128,128]{4,3,2,1,0:T(8,128)S(1)} %get-tuple-element.49), channel_id=1, source_target_pairs={{0,12},{4,0},{8,4},{12,8},{1,13},{5,1},{9,5},{13,9},{2,14},{6,2},{... | collective-permute-start | bytes 1572872 | tf_op jit(solution)/shard_map/ppermute | solution.py:22
  89.7 5.8 %collective-permute-start.13 = (f32[128,128]{1,0:T(8,128)S(1)}, f32[128,128]{1,0:T(8,128)S(1)}, u32[]{:S(2)}, u32[]{:S(2)}) collective-permute-start(f32[128,128]{1,0:T(8,128)S(1)} %get-tuple-element.51), channel_id=1, source_target_pairs={{0,16},{16,32},{32,48},{48,64},{64,80},{80,96},{96,112},{112,0},{1... | collective-permute-start | bytes 196616 | tf_op jit(solution)/shard_map/ppermute | solution.py:22
  91.7 5.0 %collective-permute-start.14 = (f32[128,128]{1,0:T(8,128)S(1)}, f32[128,128]{1,0:T(8,128)S(1)}, u32[]{:S(2)}, u32[]{:S(2)}) collective-permute-start(f32[128,128]{1,0:T(8,128)S(1)} %get-tuple-element.52), channel_id=1, source_target_pairs={{0,112},{16,0},{32,16},{48,32},{64,48},{80,64},{96,80},{112,96},{1... | collective-permute-start | bytes 196616 | tf_op jit(solution)/shard_map/ppermute | solution.py:22
  96.7 5.3 %collective-permute-start.15 = (f32[2,128,128]{2,1,0:T(8,128)S(1)}, f32[2,128,128]{2,1,0:T(8,128)S(1)}, u32[]{:S(2)}, u32[]{:S(2)}) collective-permute-start(f32[2,128,128]{2,1,0:T(8,128)S(1)} %get-tuple-element.53), channel_id=1, source_target_pairs={{0,16},{16,32},{32,48},{48,64},{64,80},{80,96},{96,112},{112,0},{1... | collective-permute-start | bytes 393224 | tf_op jit(solution)/shard_map/ppermute | solution.py:22
  99.2 6.2 %collective-permute-start.16 = (f32[2,128,128]{2,1,0:T(8,128)S(1)}, f32[2,128,128]{2,1,0:T(8,128)S(1)}, u32[]{:S(2)}, u32[]{:S(2)}) collective-permute-start(f32[2,128,128]{2,1,0:T(8,128)S(1)} %get-tuple-element.54), channel_id=1, source_target_pairs={{0,112},{16,0},{32,16},{48,32},{64,48},{80,64},{96,80},{112,96},{1... | collective-permute-start | bytes 393224 | tf_op jit(solution)/shard_map/ppermute | solution.py:22
  105.5 5.0 %collective-permute-start.20 = (f32[2,128,128]{2,1,0:T(8,128)S(1)}, f32[2,128,128]{2,1,0:T(8,128)S(1)}, u32[]{:S(2)}, u32[]{:S(2)}) collective-permute-start(f32[2,128,128]{2,1,0:T(8,128)S(1)} %get-tuple-element.55.after_ref), channel_id=1, source_target_pairs={{0,16},{16,32},{32,48},{48,64},{64,80},{80,96},{96,112},{112,0},{1... | collective-permute-start | bytes 393224 | tf_op jit(solution)/shard_map/ppermute | solution.py:22
  107.6 5.9 %collective-permute-start.21 = (f32[2,128,128]{2,1,0:T(8,128)S(1)}, f32[2,128,128]{2,1,0:T(8,128)S(1)}, u32[]{:S(2)}, u32[]{:S(2)}) collective-permute-start(f32[2,128,128]{2,1,0:T(8,128)S(1)} %get-tuple-element.60), channel_id=1, source_target_pairs={{0,112},{16,0},{32,16},{48,32},{64,48},{80,64},{96,80},{112,96},{1... | collective-permute-start | bytes 393224 | tf_op jit(solution)/shard_map/ppermute | solution.py:22
  113.5 7.0 %collective-permute-start.23 = (f32[2,128,128]{2,1,0:T(8,128)S(1)}, f32[2,128,128]{2,1,0:T(8,128)S(1)}, u32[]{:S(2)}, u32[]{:S(2)}) collective-permute-start(f32[2,128,128]{2,1,0:T(8,128)S(1)} %get-tuple-element.62), channel_id=1, source_target_pairs={{0,112},{16,0},{32,16},{48,32},{64,48},{80,64},{96,80},{112,96},{1... | collective-permute-start | bytes 393224 | tf_op jit(solution)/shard_map/ppermute | solution.py:22
  113.9 6.6 %collective-permute-start.22 = (f32[2,128,128]{2,1,0:T(8,128)S(1)}, f32[2,128,128]{2,1,0:T(8,128)S(1)}, u32[]{:S(2)}, u32[]{:S(2)}) collective-permute-start(f32[2,128,128]{2,1,0:T(8,128)S(1)} %get-tuple-element.61), channel_id=1, source_target_pairs={{0,16},{16,32},{32,48},{48,64},{64,80},{80,96},{96,112},{112,0},{1... | collective-permute-start | bytes 393224 | tf_op jit(solution)/shard_map/ppermute | solution.py:22
  116.8 6.6 %collective-permute-start.19 = (f32[2,128,128]{2,1,0:T(8,128)S(1)}, f32[2,128,128]{2,1,0:T(8,128)S(1)}, u32[]{:S(2)}, u32[]{:S(2)}) collective-permute-start(f32[2,128,128]{2,1,0:T(8,128)S(1)} %get-tuple-element.59), channel_id=1, source_target_pairs={{0,8},{4,12},{8,0},{12,4},{1,9},{5,13},{9,1},{13,5},{2,10},{6,14},... | collective-permute-start | bytes 393224 | tf_op jit(solution)/shard_map/ppermute | solution.py:22
  118.0 6.9 %collective-permute-start.18 = (f32[2,128,128]{2,1,0:T(8,128)S(1)}, f32[2,128,128]{2,1,0:T(8,128)S(1)}, u32[]{:S(2)}, u32[]{:S(2)}) collective-permute-start(f32[2,128,128]{2,1,0:T(8,128)S(1)} %get-tuple-element.58), channel_id=1, source_target_pairs={{0,12},{4,0},{8,4},{12,8},{1,13},{5,1},{9,5},{13,9},{2,14},{6,2},{... | collective-permute-start | bytes 393224 | tf_op jit(solution)/shard_map/ppermute | solution.py:22
  119.7 6.2 %collective-permute-start.17 = (f32[2,128,128]{2,1,0:T(8,128)S(1)}, f32[2,128,128]{2,1,0:T(8,128)S(1)}, u32[]{:S(2)}, u32[]{:S(2)}) collective-permute-start(f32[2,128,128]{2,1,0:T(8,128)S(1)} %get-tuple-element.57), channel_id=1, source_target_pairs={{0,4},{4,8},{8,12},{12,0},{1,5},{5,9},{9,13},{13,1},{2,6},{6,10},{... | collective-permute-start | bytes 393224 | tf_op jit(solution)/shard_map/ppermute | solution.py:22
  126.0 9.5 %collective-permute-start.25 = (bf16[2,128,128]{2,1,0:T(8,128)(2,1)S(1)}, bf16[2,128,128]{2,1,0:T(8,128)(2,1)S(1)}, u32[]{:S(2)}, u32[]{:S(2)}) collective-permute-start(bf16[2,128,128]{2,1,0:T(8,128)(2,1)S(1)} %broadcast_select_fusion), channel_id=1, source_target_pairs={{0,3},{16,19},{32,0},{48,16},{64,2},{80,18},{96,1},{112,17},{1,32}... | collective-permute-start | bytes 196616 | tf_op jit(solution)/shard_map/ppermute | solution.py:389
  132.8 11.0 %collective-permute-start.24 = (bf16[2,128,128]{2,1,0:T(8,128)(2,1)S(1)}, bf16[2,128,128]{2,1,0:T(8,128)(2,1)S(1)}, u32[]{:S(2)}, u32[]{:S(2)}) collective-permute-start(bf16[2,128,128]{2,1,0:T(8,128)(2,1)S(1)} %get-tuple-element.63), channel_id=1, source_target_pairs={{0,0},{16,16},{32,3},{48,19},{64,1},{80,17},{96,2},{112,18},{1,33}... | collective-permute-start | bytes 196616 | tf_op jit(solution)/shard_map/ppermute | solution.py:388
Sparse Core Ops, SparseCore 0:
  40.4 56.9 reduce-scatter.1
